TPU v7x, 128 devices: a whole 4x4x4 slice. The times are simulated.
128 devices in a mesh: ctx: 8 (over z, core), hr: 16 (over x, y).
Axes of the slice: x: 4, y: 4, z: 4, core: 2. Of those that a mesh axis runs over, the one named last changes fastest.
Arguments:
- token_ids: int32 [2, 8192], P(None, 'ctx'), may hold values from 0 to 32767
- embed_table: bfloat16 [32768, 4096], P(None, 'hr'), may hold values from -6 to 6
- norm_gain: bfloat16 [4096], replicated, may hold values from 0.5 to 1.5
- w_qkv: bfloat16 [4096, 16, 1, 512], P(None, 'hr'), may hold values from -0.09375 to 0.09375
- w_gate: bfloat16 [4096, 2, 8], replicated, may hold values from -0.09375 to 0.09375
- gate_bias: float32 [2, 8], replicated, may hold values from -3 to 110
- head_gain: bfloat16 [8, 512], replicated, may hold values from 0.099609375 to 1.8984375
- w_out: bfloat16 [4096, 4096], P(None, 'hr'), may hold values from -0.09375 to 0.09375
- owner: int32 [16], replicated, may hold values from 0 to 7, as said below
Outputs:
- block_out: bfloat16 [2, 8192, 4096], P(None, 'ctx', 'hr')
- memory_c: float32 [8, 16, 1, 256, 512], P('ctx', 'hr')
- memory_n: float32 [8, 16, 1, 256], P('ctx', 'hr')
- memory_m: float32 [8, 16, 1], P('ctx', 'hr')
Inputs may be any that keep to these rules, and one draw needn't show every extreme that they name: `owner`: every index along ctx owns the same number of memory groups.
All inputs are finite; a program needn't handle non-finite values.
Results may differ from a plain program's by a relative error of at most 0.01.
Values may be sent and summed in bfloat16 or wider, within the bound.
A program may use at most 128 MiB of HBM per device.

v0:
```python
import math

import jax
import jax.numpy as jnp
from jax import lax
from jax.sharding import PartitionSpec as P

very_negative = -1e30
epsilon = 1e-06


def swapped(value, axis, distance):
    mask = 2**distance
    pairs = [(source, source ^ mask) for source in range(lax.axis_size(axis))]
    return lax.ppermute(value, axis, pairs)


def passed_along(value, axis, steps):
    count = lax.axis_size(axis)
    leading, last = (max(0, -steps), min(count, count - steps))
    return lax.ppermute(value, axis, [(source, source + steps) for source in range(leading, last)])


def from_root(value, axis, root):
    mine = lax.axis_index(axis) == root
    return lax.psum(jnp.where(mine, value, jnp.zeros_like(value)), axis)


def combine(earlier, later):
    decay_one, max_one, memory_one, norm_one = earlier
    decay_two, max_two, memory_two, norm_two = later
    joined = jnp.maximum(decay_two + max_one, max_two)
    first_w = jnp.exp(decay_two + max_one - joined)
    second_w = jnp.exp(max_two - joined)
    memory = first_w[..., None, None] * memory_one + second_w[..., None, None] * memory_two
    normer = first_w[..., None] * norm_one + second_w[..., None] * norm_two
    return (decay_one + decay_two, joined, memory, normer)


def block_pass(queries, key_rows, values, in_gate, log_forget):
    length = queries.shape[0]
    inv_root = 1.0 / math.sqrt(queries.shape[1])
    cumulative = jnp.cumsum(log_forget)
    total_decay = cumulative[-1]
    causal_mask = lax.broadcasted_iota(jnp.int32, (length, length), 0) >= lax.broadcasted_iota(
        jnp.int32, (length, length), 1
    )
    exponent = jnp.where(
        causal_mask, cumulative[:, None] - cumulative[None, :] + in_gate[None, :], very_negative
    )
    local_max = jnp.max(exponent, axis=1)
    weights = jnp.exp(exponent - local_max[:, None])
    scores = jnp.dot(queries, key_rows.T, preferred_element_type=jnp.float32) * inv_root
    weighted = weights * scores
    numerator = jnp.dot(weighted.astype(jnp.bfloat16), values, preferred_element_type=jnp.float32)
    denominator = jnp.sum(weighted, axis=1)
    tail_decay = total_decay - cumulative + in_gate
    block_max = jnp.max(tail_decay)
    scaled_keys = key_rows.astype(jnp.float32) * jnp.exp(tail_decay - block_max)[:, None]
    block_memory = jnp.dot(
        scaled_keys.astype(jnp.bfloat16).T, values, preferred_element_type=jnp.float32
    )
    block_norm = jnp.sum(scaled_keys, axis=0)
    return (
        numerator,
        denominator,
        local_max,
        cumulative,
        (total_decay, block_max, block_memory, block_norm),
    )


def finish(numerator, denominator, local_max, cumulative, state, queries):
    decay_in, max_in, memory_in, norm_in = state
    inv_root = 1.0 / math.sqrt(queries.shape[1])
    row_max = jnp.maximum(cumulative + max_in, local_max)
    inner = jnp.exp(local_max - row_max)
    outer = jnp.exp(cumulative + max_in - row_max)
    scaled_q = queries.astype(jnp.float32) * inv_root
    carried = (
        jnp.dot(queries, memory_in.astype(jnp.bfloat16), preferred_element_type=jnp.float32)
        * inv_root
    )
    top = inner[:, None] * numerator + outer[:, None] * carried
    bottom = inner * denominator + outer * jnp.dot(
        scaled_q, norm_in, precision=lax.Precision.HIGHEST
    )
    return top / jnp.maximum(jnp.abs(bottom), jnp.exp(-row_max))[:, None]


def local(token_ids, embed_table, norm_gain, w_qkv, w_gate, gate_bias, head_gain, w_out, owner):
    hr_index = lax.axis_index("hr")
    ctx_index = lax.axis_index("ctx")
    hr_count = lax.axis_size("hr")
    ctx_count = lax.axis_size("ctx")
    request_count, token_count = token_ids.shape
    local_width = embed_table.shape[1]
    heads_here = w_qkv.shape[2]
    pair_width = w_qkv.shape[3]
    key_width = pair_width // 2
    head_total = gate_bias.shape[1]
    which_part = hr_index % 2
    head_group = hr_index // 2
    first_part = which_part == 0
    embedded = embed_table[token_ids]
    w_mine = w_qkv[:, 0]
    model_width = w_mine.shape[0]
    w_flat = w_mine.reshape(model_width, heads_here * pair_width)
    gate_flat = w_gate.reshape(model_width, 2 * head_total)
    wide_local = embedded.astype(jnp.float32)
    square_sums = lax.psum(jnp.sum(wide_local * wide_local, axis=2), "hr")
    row_scale = lax.rsqrt(square_sums / (local_width * hr_count) + epsilon)
    gain_local = lax.dynamic_slice_in_dim(norm_gain, hr_index * local_width, local_width, 0).astype(
        jnp.float32
    )
    normed_local = (wide_local * row_scale[..., None] * gain_local).astype(jnp.bfloat16)
    piece = lax.all_gather(normed_local, "hr", axis=2, tiled=True)
    projected = jnp.einsum("rtc,cn->rtn", piece, w_flat, preferred_element_type=jnp.float32)
    gates_all = jnp.einsum("rtc,cn->rtn", piece, gate_flat, preferred_element_type=jnp.float32)
    projected = projected.astype(jnp.bfloat16).reshape(
        request_count, token_count, heads_here, pair_width
    )
    own_part = jnp.where(first_part, projected[0], projected[1])
    other_part = jnp.where(first_part, projected[1], projected[0])
    partner_part = swapped(other_part, "hr", 0)
    gates = jnp.where(first_part, gates_all[0], gates_all[1])
    query_key = jnp.where(first_part, own_part, partner_part)
    value_rows = jnp.where(first_part, partner_part, own_part)
    gate_pick = lax.dynamic_slice_in_dim(
        gates.reshape(token_count, 2, head_total), head_group * heads_here, heads_here, 2
    )
    bias_pick = lax.dynamic_slice_in_dim(gate_bias, head_group * heads_here, heads_here, 1)
    gate_pre = gate_pick + bias_pick[None]
    block_len = min(token_count, 512)
    block_count = token_count // block_len
    queries = query_key[..., :key_width].reshape(block_count, block_len, heads_here, key_width)
    key_rows = query_key[..., key_width:].reshape(block_count, block_len, heads_here, key_width)
    values = value_rows.reshape(block_count, block_len, heads_here, pair_width)
    gate_in = gate_pre[:, 0].reshape(block_count, block_len, heads_here)
    gate_forget = jax.nn.log_sigmoid(gate_pre[:, 1]).reshape(block_count, block_len, heads_here)
    per_head = jax.vmap(block_pass, in_axes=(1, 1, 1, 1, 1))
    per_block = jax.vmap(per_head, in_axes=(0, 0, 0, 0, 0))
    numerator, denominator, local_max, cumulative, summary = per_block(
        queries, key_rows, values, gate_in, gate_forget
    )
    identity = (
        jnp.zeros((heads_here,), jnp.float32),
        jnp.full((heads_here,), very_negative, jnp.float32),
        jnp.zeros((heads_here, key_width, pair_width), jnp.float32),
        jnp.zeros((heads_here, key_width), jnp.float32),
    )

    def advance(state, piece):
        return (combine(state, piece), state)

    device_summary, entering = lax.scan(advance, identity, summary)
    prefix = identity
    inclusive = device_summary

    def keep_first(start_leaf, got_leaf):
        return jnp.where(ctx_index == 0, start_leaf, got_leaf)

    for section in range(ctx_count - 1):
        arrived = passed_along((inclusive[0], inclusive[1], inclusive[2], inclusive[3]), "ctx", 1)
        prefix = jax.tree.map(keep_first, identity, arrived)
        inclusive = combine(prefix, device_summary)

    def add_lead(leaf):
        return leaf[None]

    starts = combine(jax.tree.map(add_lead, prefix), entering)
    finish_head = jax.vmap(finish, in_axes=(0, 0, 0, 0, 0, 1))
    finish_block = jax.vmap(finish_head, in_axes=(0, 0, 0, 0, 0, 0))
    hidden = finish_block(numerator, denominator, local_max, cumulative, starts, queries)
    hidden = jnp.transpose(hidden, (1, 0, 2, 3)).reshape(heads_here, token_count, pair_width)
    gain_pick = lax.dynamic_slice_in_dim(head_gain, head_group * heads_here, heads_here, 0).astype(
        jnp.float32
    )
    head_normed = (
        hidden
        * lax.rsqrt(jnp.mean(hidden * hidden, axis=-1, keepdims=True) + epsilon)
        * gain_pick[:, None, :]
    ).astype(jnp.bfloat16)
    w_heads = w_out.reshape(head_total, pair_width, local_width)
    head_ids = lax.broadcasted_iota(jnp.int32, (1, head_total), 1)
    request_ids = lax.broadcasted_iota(jnp.int32, (1, request_count), 1)
    piece = lax.all_gather(head_normed, "hr", axis=0, tiled=True)
    count = piece.shape[0]
    rows = lax.broadcasted_iota(jnp.int32, (count, 1), 0)
    source = rows // heads_here
    head_of = source // 2 * heads_here + rows % heads_here
    request_of = source % 2
    pick_head = (head_of == head_ids).astype(jnp.bfloat16)
    chosen = jnp.einsum(
        "kn,ncd->kcd", pick_head, w_heads, preferred_element_type=jnp.float32
    ).astype(jnp.bfloat16)
    partial_out = jnp.einsum("ktc,kcd->ktd", piece, chosen, preferred_element_type=jnp.float32)
    pick_request = (request_of == request_ids).astype(jnp.float32)
    mixed = jnp.einsum("ktd,kr->rtd", partial_out, pick_request)
    block_out = (embedded.astype(jnp.float32) + mixed).astype(jnp.bfloat16)
    final_state = combine(prefix, device_summary)
    handed = (
        from_root(final_state[2].astype(jnp.bfloat16), "ctx", ctx_count - 1).astype(jnp.float32),
        from_root(final_state[3].astype(jnp.bfloat16), "ctx", ctx_count - 1).astype(jnp.float32),
        from_root(final_state[1].astype(jnp.bfloat16), "ctx", ctx_count - 1).astype(jnp.float32),
    )
    owner_here = lax.dynamic_slice_in_dim(owner, hr_index, 1, 0)[0]
    keep = (owner_here == ctx_index).astype(jnp.float32)
    memory_c = (keep * handed[0])[None, None]
    memory_n = (keep * handed[1])[None, None]
    memory_m = (keep * handed[2])[None, None]
    return (block_out, memory_c, memory_n, memory_m)


def solution(mesh):
    return jax.shard_map(
        local,
        mesh=mesh,
        in_specs=(
            P(None, "ctx"),
            P(None, "hr"),
            P(),
            P(None, "hr", None, None),
            P(),
            P(),
            P(),
            P(None, "hr"),
            P(),
        ),
        out_specs=(
            P(None, "ctx", "hr"),
            P("ctx", "hr", None, None, None),
            P("ctx", "hr", None, None),
            P("ctx", "hr", None),
        ),
        check_vma=False,
    )
```

profile of v0, /device:TPU:8, one launch (start us, length us, event | category | flops | bytes accessed | tf_op | source)
XLA Modules:
  0.0 556.8 jit_solution(3451547791221327625)
XLA Ops:
  8.1 16.4 %gather_fusion = bf16[2048,256]{1,0:T(8,128)(2,1)} fusion(bf16[32768,256]{1,0:T(8,128)(2,1)} %param.12, s32[2048]{0:T(1024)S(1)} %bitcast_clamp_fusion), kind=kCustom, calls=%fused_computation | custom fusion | bytes 2105344 | tf_op jit(solution)/shard_map/gather | solution.py:105
  24.5 1.6 fusion.9
  26.1 37.0 %psum.28 = f32[2,1024]{1,0:T(2,128)S(1)} all-reduce(f32[2,1024]{1,0:T(2,128)S(1)} %fusion.9), channel_id=1, replica_groups=mesh['ctx'=8,'hr'=16] {'hr'}, use_global_device_ids=true, to_apply=%region_1.2 | all-reduce | flops 2048 | bytes 16384 | tf_op jit(solution)/shard_map/psum | solution.py:111
  63.9 2.6 fusion.11
  66.9 121.7 %all-gather.3.cloned.1.call-done = bf16[2,1024,4096]{2,1,0:T(8,128)(2,1)} async-done(((bf16[2,1024,256]{2,1,0:T(8,128)(2,1)}), bf16[2,1024,4096]{2,1,0:T(8,128)(2,1)}) %all-gather.3.cloned.1.call-update) | async-done | bytes 16777232 | tf_op jit(solution)/shard_map/all_gather | solution.py:117
  188.6 10.3 %fusion.32 = f32[2,1024,16]{1,2,0:T(8,128)S(1)} fusion(bf16[2,1024,4096]{2,1,0:T(8,128)(2,1)} %all-gather.3.cloned.1.call-done, bf16[4096,2,8]{0,2,1:T(8,128)(2,1)S(1)} %copy-done.8), kind=kOutput, calls=%fused_computation.64 | convolution fusion | flops 268435456 | bytes 17039360 | tf_op jit(solution)/shard_map/rtc,cn->rtn/dot_general | solution.py:119
  199.1 1.2 copy-done.10
  200.3 9.0 %fusion.16 = bf16[2,1024,512]{2,1,0:T(8,128)(2,1)S(1)} fusion(bf16[2,1024,4096]{2,1,0:T(8,128)(2,1)S(1)} %copy-done.1, bf16[4096,1,1,512]{3,0,2,1:T(8,128)(2,1)S(1)} %copy-done.10), kind=kOutput, calls=%fused_computation.33 | convolution fusion | flops 8590983168 | bytes 23068672 | tf_op jit(solution)/shard_map/rtc,cn->rtn/dot_general | solution.py:118
  209.3 1.3 copy-done.5
  214.3 21.8 %collective-permute-done = bf16[1024,1,512]{2,0,1:T(8,128)(2,1)} collective-permute-done((bf16[1024,1,512]{2,0,1:T(8,128)(2,1)}, bf16[1024,1,512]{2,0,1:T(8,128)(2,1)}, u32[]{:S(2)}, u32[]{:S(2)}) %collective-permute-start) | collective-permute-done | bytes 1048608 | tf_op jit(solution)/shard_map/ppermute | solution.py:15
  236.0 3.0 bitcast_select_fusion.1
  239.0 1.1 slice_convert_fusion
  241.4 2.5 copy.46
  243.9 3.0 convolution_bitcast_fusion
  246.9 11.0 %while.25 = (s32[]{:T(128)}, f32[1]{0:T(128)}, f32[1]{0:T(128)}, f32[1,256,512]{2,1,0:T(8,128)S(1)}, f32[1,256]{1,0:T(1,128)S(1)}, /*index=5*/f32[2,1]{0,1:T(1,1...) while((s32[]{:T(128)}, f32[1]{0:T(128)}, f32[1]{0:T(128)}, ...), condition=%wide.region_8.9_spmd.clone, body=%wide.region_7.8_spmd.clone.sunk | while | flops 656648 | bytes 2626874 | solution.py:156
  250.9 1.4 bitcast_add_fusion.4
  256.5 1.4 bitcast_add_fusion.4
  257.9 1.3 collective-permute-start.8
  259.2 5.0 collective-permute-start.1
  265.8 6.1 %collective-permute-start.9 = (f32[1,256,512]{2,1,0:T(8,128)}, f32[1,256,512]{2,1,0:T(8,128)}, u32[]{:S(2)}, u32[]{:S(2)}) collective-permute-start(f32[1,256,512]{2,1,0:T(8,128)} %multiply_add_fusion.5), channel_id=1, source_target_pairs={{0,16},{16,32},{32,48},{48,64},{64,80},{80,96},{96,112},{1,17},{17... | collective-permute-start | bytes 1572872 | tf_op jit(solution)/shard_map/ppermute | solution.py:21
  272.4 4.6 collective-permute-start.2
  277.9 5.9 %collective-permute-start.10 = (f32[1,256,512]{2,1,0:T(8,128)S(1)}, f32[1,256,512]{2,1,0:T(8,128)S(1)}, u32[]{:S(2)}, u32[]{:S(2)}) collective-permute-start(f32[1,256,512]{2,1,0:T(8,128)S(1)} %multiply_add_fusion.4), channel_id=1, source_target_pairs={{0,16},{16,32},{32,48},{48,64},{64,80},{80,96},{96,112},{1,17},{17... | collective-permute-start | bytes 1572872 | tf_op jit(solution)/shard_map/ppermute | solution.py:21
  284.6 4.4 collective-permute-start.15
  289.6 2.9 collective-permute-start.3
  293.2 3.3 collective-permute-start.16
  296.6 4.3 collective-permute-start.11
  301.9 3.0 collective-permute-start.4
  305.6 4.1 collective-permute-start.17
  309.8 4.5 collective-permute-start.12
  315.1 2.7 collective-permute-start.5
  317.8 4.6 collective-permute-start.18
  323.0 2.7 collective-permute-start.6
  326.5 4.1 collective-permute-start.7
  331.4 3.8 collective-permute-start.19
  335.3 4.3 collective-permute-start.13
  339.6 1.9 collective-permute-start.20
  342.3 5.3 collective-permute-start.21
  347.8 4.4 collective-permute-start.14
  353.8 2.1 multiply_reduce_fusion
  356.8 2.8 fusion.14
  360.9 3.2 convolution_convert_fusion
  364.1 17.7 %all-reduce = (bf16[1,256]{1,0:T(2,128)(2,1)S(1)}, bf16[1]{0:T(256)(128)(2,1)}) all-reduce(bf16[1,256]{1,0:T(2,128)(2,1)S(1)} %get-tuple-element.208, bf16[1]{0:T(256)(128)(2,1)S(6)} %select_n.314), channel_id=1, replica_groups=mesh['ctx'=8,'hr'=16] {'ctx'}, use_global_device_ids=true, to_apply=%region_12.13 | all-reduce | flops 257 | bytes 1028 | tf_op jit(solution)/shard_map/psum | solution.py:26
  383.1 37.9 %all-reduce.3.cloned.1.call-done = bf16[1,256,512]{2,1,0:T(8,128)(2,1)} async-done(((bf16[1,256,512]{2,1,0:T(8,128)(2,1)}), bf16[1,256,512]{2,1,0:T(8,128)(2,1)}) %all-reduce.3.cloned.1.call-update) | async-done | bytes 262160 | tf_op jit(solution)/shard_map/psum | solution.py:26
  421.0 1.8 multiply_bitcast_fusion
  422.8 110.7 %all-gather.5.cloned.1.call-done = bf16[16,1024,512]{2,1,0:T(8,128)(2,1)} async-done(((bf16[1,1024,512]{2,1,0:T(8,128)(2,1)}), bf16[16,1024,512]{2,1,0:T(8,128)(2,1)}) %all-gather.5.cloned.1.call-update) | async-done | bytes 16777232 | tf_op jit(solution)/shard_map/all_gather | solution.py:187
  533.5 9.5 %fusion.7 = bf16[16,1024,256]{2,1,0:T(8,128)(2,1)S(1)} fusion(bf16[16,1024,512]{2,1,0:T(8,128)(2,1)} %all-gather.5.cloned.1.call-done, bf16[16,512,256]{2,0,1:T(8,128)(2,1)} %convolution_convert_fusion), kind=kOutput, calls=%fused_computation.15 | convolution fusion | flops 4294967296 | bytes 29360128 | tf_op jit(solution)/shard_map/ktc,kcd->ktd/dot_general | solution.py:197
  543.0 4.9 fusion.3
  547.9 1.3 fusion.12
  (127 shorter events, 19.6 us)
Async XLA Ops:
  7.2 353.7 %copy-start = (bf16[4096,256]{1,0:T(8,128)(2,1)S(1)}, bf16[4096,256]{1,0:T(8,128)(2,1)}, u32[]{:S(2)}) copy-start(bf16[4096,256]{1,0:T(8,128)(2,1)} %param.18) | copy-start | bytes 6291460
  7.2 181.4 %all-gather.3.cloned.1.call-start = ((), (), s32[]{:S(2)}) async-start(), calls=%async_computation | async-start | bytes 17825792 | tf_op jit(solution)/shard_map/all_gather | solution.py:117
  24.5 42.2 %copy-start.9 = (f32[2,8]{1,0:T(2,128)S(1)}, f32[2,8]{1,0:T(2,128)}, u32[]{:S(2)}) copy-start(f32[2,8]{1,0:T(2,128)} %param.16) | copy-start | bytes 196
  24.5 164.1 %copy-start.8 = (bf16[4096,2,8]{0,2,1:T(8,128)(2,1)S(1)}, bf16[4096,2,8]{0,2,1:T(8,128)(2,1)}, u32[]{:S(2)}) copy-start(bf16[4096,2,8]{0,2,1:T(8,128)(2,1)} %param.15) | copy-start | bytes 393220
  66.5 354.5 %all-reduce.3.cloned.1.call-start = ((), (), s32[]{:S(2)}) async-start(), calls=%async_computation.2 | async-start | bytes 524288 | tf_op jit(solution)/shard_map/psum | solution.py:26
  188.6 10.5 %copy-start.1 = (bf16[2,1024,4096]{2,1,0:T(8,128)(2,1)S(1)}, bf16[2,1024,4096]{2,1,0:T(8,128)(2,1)}, u32[]{:S(2)}) copy-start(bf16[2,1024,4096]{2,1,0:T(8,128)(2,1)} %all-gather.3.cloned.1.call-done) | copy-start | bytes 50331652
  188.6 11.7 %copy-start.10 = (bf16[4096,1,1,512]{3,0,2,1:T(8,128)(2,1)S(1)}, bf16[4096,1,1,512]{3,0,2,1:T(8,128)(2,1)}, u32[]{:S(2)}) copy-start(bf16[4096,1,1,512]{3,0,2,1:T(8,128)(2,1)} %param.14) | copy-start | bytes 12582916
  209.3 1.3 copy-start.5
  211.7 24.3 %collective-permute-start = (bf16[1024,1,512]{2,0,1:T(8,128)(2,1)}, bf16[1024,1,512]{2,0,1:T(8,128)(2,1)}, u32[]{:S(2)}, u32[]{:S(2)}) collective-permute-start(bf16[1024,1,512]{2,0,1:T(8,128)(2,1)} %select_bitcast_fusion), channel_id=1, source_target_pairs={{0,1},{1,0},{2,3},{3,2},{4,5},{5,4},{6,7},{7,6},{8,9},{9,8},{10,11... | collective-permute-start | bytes 3145736 | tf_op jit(solution)/shard_map/ppermute | solution.py:15
  240.2 1.0 copy-start.3
  257.9 7.0 %collective-permute-start.8 = (f32[1,256,512]{2,1,0:T(8,128)S(1)}, f32[1,256,512]{2,1,0:T(8,128)S(1)}, u32[]{:S(2)}, u32[]{:S(2)}) collective-permute-start(f32[1,256,512]{2,1,0:T(8,128)S(1)} %get-tuple-element.82), channel_id=1, source_target_pairs={{0,16},{16,32},{32,48},{48,64},{64,80},{80,96},{96,112},{1,17},{17... | collective-permute-start | bytes 1572872 | tf_op jit(solution)/shard_map/ppermute | solution.py:21
  259.2 5.0 collective-permute-start.1
  265.8 12.0 %collective-permute-start.9 = (f32[1,256,512]{2,1,0:T(8,128)}, f32[1,256,512]{2,1,0:T(8,128)}, u32[]{:S(2)}, u32[]{:S(2)}) collective-permute-start(f32[1,256,512]{2,1,0:T(8,128)} %multiply_add_fusion.5), channel_id=1, source_target_pairs={{0,16},{16,32},{32,48},{48,64},{64,80},{80,96},{96,112},{1,17},{17... | collective-permute-start | bytes 1572872 | tf_op jit(solution)/shard_map/ppermute | solution.py:21
  272.4 28.5 %copy-start.6 = (bf16[1024,1,256]{2,0,1:T(8,128)(2,1)S(1)}, bf16[1024,1,256]{2,0,1:T(8,128)(2,1)}, u32[]{:S(2)}) copy-start(bf16[1024,1,256]{2,0,1:T(8,128)(2,1)} %get-tuple-element.217) | copy-start | bytes 1572868
  272.4 28.5 %copy-start.7 = (bf16[1024,1,256]{2,0,1:T(8,128)(2,1)S(1)}, bf16[1024,1,256]{2,0,1:T(8,128)(2,1)}, u32[]{:S(2)}) copy-start(bf16[1024,1,256]{2,0,1:T(8,128)(2,1)} %get-tuple-element.218) | copy-start | bytes 1572868
  272.4 4.6 collective-permute-start.2
  277.9 18.6 %collective-permute-start.10 = (f32[1,256,512]{2,1,0:T(8,128)S(1)}, f32[1,256,512]{2,1,0:T(8,128)S(1)}, u32[]{:S(2)}, u32[]{:S(2)}) collective-permute-start(f32[1,256,512]{2,1,0:T(8,128)S(1)} %multiply_add_fusion.4), channel_id=1, source_target_pairs={{0,16},{16,32},{32,48},{48,64},{64,80},{80,96},{96,112},{1,17},{17... | collective-permute-start | bytes 1572872 | tf_op jit(solution)/shard_map/ppermute | solution.py:21
  284.6 8.6 %collective-permute-start.15 = (f32[1,256]{1,0:T(1,128)S(1)}, f32[1,256]{1,0:T(1,128)S(1)}, u32[]{:S(2)}, u32[]{:S(2)}) collective-permute-start(f32[1,256]{1,0:T(1,128)S(1)} %get-tuple-element.84), channel_id=1, source_target_pairs={{0,16},{16,32},{32,48},{48,64},{64,80},{80,96},{96,112},{1,17},{17... | collective-permute-start | bytes 3080 | tf_op jit(solution)/shard_map/ppermute | solution.py:21
  289.6 2.9 collective-permute-start.3
  293.2 12.4 %collective-permute-start.16 = (f32[1,256]{1,0:T(1,128)S(1)}, f32[1,256]{1,0:T(1,128)S(1)}, u32[]{:S(2)}, u32[]{:S(2)}) collective-permute-start(f32[1,256]{1,0:T(1,128)S(1)} %fusion.51), channel_id=1, source_target_pairs={{0,16},{16,32},{32,48},{48,64},{64,80},{80,96},{96,112},{1,17},{17... | collective-permute-start | bytes 3080 | tf_op jit(solution)/shard_map/ppermute | solution.py:21
  296.6 13.0 %collective-permute-start.11 = (f32[1,256,512]{2,1,0:T(8,128)S(1)}, f32[1,256,512]{2,1,0:T(8,128)S(1)}, u32[]{:S(2)}, u32[]{:S(2)}) collective-permute-start(f32[1,256,512]{2,1,0:T(8,128)S(1)} %multiply_add_fusion.3), channel_id=1, source_target_pairs={{0,16},{16,32},{32,48},{48,64},{64,80},{80,96},{96,112},{1,17},{17... | collective-permute-start | bytes 1572872 | tf_op jit(solution)/shard_map/ppermute | solution.py:21
  301.9 12.4 %copy-start.4 = (bf16[1024,1,512]{2,0,1:T(8,128)(2,1)S(1)}, bf16[1024,1,512]{2,0,1:T(8,128)(2,1)}, u32[]{:S(2)}) copy-start(bf16[1024,1,512]{2,0,1:T(8,128)(2,1)} %get-tuple-element.215) | copy-start | bytes 3145732
  301.9 3.0 collective-permute-start.4
  305.6 12.2 %collective-permute-start.17 = (f32[1,256]{1,0:T(1,128)S(1)}, f32[1,256]{1,0:T(1,128)S(1)}, u32[]{:S(2)}, u32[]{:S(2)}) collective-permute-start(f32[1,256]{1,0:T(1,128)S(1)} %fusion.53), channel_id=1, source_target_pairs={{0,16},{16,32},{32,48},{48,64},{64,80},{80,96},{96,112},{1,17},{17... | collective-permute-start | bytes 3080 | tf_op jit(solution)/shard_map/ppermute | solution.py:21
  309.8 25.4 %collective-permute-start.12 = (f32[1,256,512]{2,1,0:T(8,128)S(1)}, f32[1,256,512]{2,1,0:T(8,128)S(1)}, u32[]{:S(2)}, u32[]{:S(2)}) collective-permute-start(f32[1,256,512]{2,1,0:T(8,128)S(1)} %multiply_add_fusion.2), channel_id=1, source_target_pairs={{0,16},{16,32},{32,48},{48,64},{64,80},{80,96},{96,112},{1,17},{17... | collective-permute-start | bytes 1572872 | tf_op jit(solution)/shard_map/ppermute | solution.py:21
  315.1 7.3 %collective-permute-start.5 = (f32[1]{0:T(128)}, f32[1]{0:T(128)}, u32[]{:S(2)}, u32[]{:S(2)}) collective-permute-start(f32[1]{0:T(128)} %max.69), channel_id=1, source_target_pairs={{0,16},{16,32},{32,48},{48,64},{64,80},{80,96},{96,112},{1,17},{17... | collective-permute-start | bytes 20 | tf_op jit(solution)/shard_map/ppermute | solution.py:21
  317.8 13.5 %collective-permute-start.18 = (f32[1,256]{1,0:T(1,128)S(1)}, f32[1,256]{1,0:T(1,128)S(1)}, u32[]{:S(2)}, u32[]{:S(2)}) collective-permute-start(f32[1,256]{1,0:T(1,128)S(1)} %fusion.55), channel_id=1, source_target_pairs={{0,16},{16,32},{32,48},{48,64},{64,80},{80,96},{96,112},{1,17},{17... | collective-permute-start | bytes 3080 | tf_op jit(solution)/shard_map/ppermute | solution.py:21
  323.0 2.8 collective-permute-start.6
  326.5 4.2 collective-permute-start.7
  331.4 8.3 %collective-permute-start.19 = (f32[1,256]{1,0:T(1,128)S(1)}, f32[1,256]{1,0:T(1,128)S(1)}, u32[]{:S(2)}, u32[]{:S(2)}) collective-permute-start(f32[1,256]{1,0:T(1,128)S(1)} %fusion.57), channel_id=1, source_target_pairs={{0,16},{16,32},{32,48},{48,64},{64,80},{80,96},{96,112},{1,17},{17... | collective-permute-start | bytes 3080 | tf_op jit(solution)/shard_map/ppermute | solution.py:21
  335.2 18.6 %copy-start.11 = (f32[2,1,256,512]{3,2,1,0:T(8,128)S(1)}, f32[2,1,256,512]{3,2,1,0:T(8,128)}, u32[]{:S(2)}) copy-start(f32[2,1,256,512]{3,2,1,0:T(8,128)} %get-tuple-element.83) | copy-start | bytes 3145732
  335.3 12.4 %collective-permute-start.13 = (f32[1,256,512]{2,1,0:T(8,128)S(1)}, f32[1,256,512]{2,1,0:T(8,128)S(1)}, u32[]{:S(2)}, u32[]{:S(2)}) collective-permute-start(f32[1,256,512]{2,1,0:T(8,128)S(1)} %multiply_add_fusion.1), channel_id=1, source_target_pairs={{0,16},{16,32},{32,48},{48,64},{64,80},{80,96},{96,112},{1,17},{17... | collective-permute-start | bytes 1572872 | tf_op jit(solution)/shard_map/ppermute | solution.py:21
  339.6 2.7 collective-permute-start.20
  342.3 9.9 %collective-permute-start.21 = (f32[1,256]{1,0:T(1,128)S(1)}, f32[1,256]{1,0:T(1,128)S(1)}, u32[]{:S(2)}, u32[]{:S(2)}) collective-permute-start(f32[1,256]{1,0:T(1,128)S(1)} %fusion.61), channel_id=1, source_target_pairs={{0,16},{16,32},{32,48},{48,64},{64,80},{80,96},{96,112},{1,17},{17... | collective-permute-start | bytes 3080 | tf_op jit(solution)/shard_map/ppermute | solution.py:21
  347.8 5.9 %collective-permute-start.14 = (f32[1,256,512]{2,1,0:T(8,128)S(1)}, f32[1,256,512]{2,1,0:T(8,128)S(1)}, u32[]{:S(2)}, u32[]{:S(2)}) collective-permute-start(f32[1,256,512]{2,1,0:T(8,128)S(1)} %multiply_add_fusion), channel_id=1, source_target_pairs={{0,16},{16,32},{32,48},{48,64},{64,80},{80,96},{96,112},{1,17},{17... | collective-permute-start | bytes 1572872 | tf_op jit(solution)/shard_map/ppermute | solution.py:21
  356.7 176.8 %all-gather.5.cloned.1.call-start = ((), (), s32[]{:S(2)}) async-start(), calls=%async_computation.1 | async-start | bytes 17825792 | tf_op jit(solution)/shard_map/all_gather | solution.py:187
  356.8 2.9 copy-start.12
  543.0 4.9 copy-start.2
Sparse Core Ops, SparseCore 0:
  66.6 121.8 all-gather.2
  356.8 64.0 all-reduce.2
  423.4 110.0 all-gather.4
where the time goes:
time: 559 us; the launch traced here: 557 us
  waiting for transfers between devices  293 us (52%)
  starting transfers between devices  84.2 us (15%)
  blocking collectives  54.8 us (10%)
  matrix products  44.7 us (8%)
  other arithmetic  27.3 us (5%)
  local copies, waits for them, and re-layouts  25.9 us (5%)
  between operations  21.8 us (4%)
    all_gather x1, waiting for transfers between devices, local(): piece = lax.all_gather(normed_local, 'hr', axis=2, tiled=True)  122 us
    all_gather x1, waiting for transfers between devices, local(): piece = lax.all_gather(head_normed, 'hr', axis=0, tiled=True)  111 us
    ppermute x21, starting transfers between devices, passed_along(): lax.ppermute(value, axis, [(source, source + steps) for source in range(l...  83.2 us
    psum x1, waiting for transfers between devices, from_root(): return lax.psum(jnp.where(mine, value, jnp.zeros_like(value)), axis)  37.9 us
    psum x1, blocking collectives, local(): square_sums = lax.psum(jnp.sum(wide_local * wide_local, axis=2), 'hr')  37 us
    ppermute x1, waiting for transfers between devices, swapped(): return lax.ppermute(value, axis, pairs)  21.8 us
    psum x1, blocking collectives, from_root(): return lax.psum(jnp.where(mine, value, jnp.zeros_like(value)), axis)  17.7 us
    gather x1, local copies, waits for them, and re-layouts, local(): embedded = embed_table[token_ids]  16.4 us
  transfers between devices with their start and end apart: 25, of which 6 were waited for; matrix products, arithmetic and copies ran while one was open for 3% of the time, Pallas kernels for 0%

commit v1 on v0

v1 whole, which is shorter than its diff:
```python
import jax
import jax.numpy as jnp
from jax import lax
from jax.experimental import pallas as pl
from jax.experimental.pallas import tpu as pltpu
from jax.sharding import PartitionSpec as P

MESH = pl.DeviceIdType.MESH
F32 = jnp.float32
BF16 = jnp.bfloat16
very_negative = -1e30
epsilon = 1e-06

WIDTH = 4096
ROWS = 1024
HALF = 512
PIECES = 2
PIECE = HALF // PIECES
KEY = 256
VAL = 512
SENDS = 96


def dot(a, b):
    return jnp.dot(a, b, preferred_element_type=F32)


def kernel(
    emb,
    w_own,
    w_out,
    w_gate,
    bias,
    gain,
    out_rows,
    out_mem,
    out_aux,
    xb,
    wb,
    wo,
    qs,
    ks,
    vs,
    gs,
    num,
    den,
    rows_in,
    cols_in,
    sum_c,
    sum_aux,
    state_c,
    hn,
    act,
    opp,
    right_p,
    left_p,
    own_p,
    opp_in,
    right_in,
    left_in,
    total,
    mem_out,
    aux_out,
    send_sem,
    local_sem,
    sem_a,
    sem_ring,
    sem_sib,
    sem_w,
    sem_wz,
    sem_wo,
    sem_woz,
    sem_state,
    sem_hn,
    sem_red,
    sem_out,
    sem_mem,
):
    c = lax.axis_index("ctx")
    h = lax.axis_index("hr")
    x, y = h // 4, h % 4
    z, k = c // 2, c % 2
    req, par = y // 2, y % 2

    def dev(x_, y_, z_, k_):
        return (z_ * 2 + k_, x_ * 4 + y_)

    def rel(base, step):
        return lax.rem(base + step, 4)

    sib = dev(x, y, z, 1 - k)
    x_next, x_prev = dev(rel(x, 1), y, z, k), dev(rel(x, 3), y, z, k)
    z_next, z_prev = dev(x, y, rel(z, 1), k), dev(x, y, rel(z, 3), k)
    y_mate = 2 * req + 1 - par

    partners = [sib]
    for step in (1, 2, 3):
        for core in (0, 1):
            partners.append(dev(x, rel(y, step), z, core))
        partners.append(dev(rel(x, step), y, z, k))
        partners.append(dev(x, y, rel(z, step), k))
        partners.append(dev(x, y_mate, rel(z, step), k))
    barrier = pltpu.get_barrier_semaphore()
    for partner in partners:
        pl.semaphore_signal(barrier, inc=1, device_id=partner, device_id_type=MESH)
    pl.semaphore_wait(barrier, len(partners))

    pending = []

    def push(src, dst, sem, target, when=None):
        slot = len(pending)
        copy = pltpu.make_async_remote_copy(
            src_ref=src,
            dst_ref=dst,
            send_sem=send_sem.at[slot],
            recv_sem=sem,
            device_id=target,
            device_id_type=MESH,
        )
        pending.append((copy, when))
        if when is None:
            copy.start()
        else:
            pl.when(when)(copy.start)

    def here(src, dst, sem, when):
        copy = pltpu.make_async_copy(src, dst, sem)
        pl.when(when)(copy.start)

    def arrived(dst, sem):
        pltpu.make_async_remote_copy(
            src_ref=dst,
            dst_ref=dst,
            send_sem=send_sem.at[0],
            recv_sem=sem,
            device_id=sib,
            device_id_type=MESH,
        ).wait_recv()

    k_half = k * HALF

    for piece in range(PIECES):
        for r_ in (0, 1):
            for kd in (0, 1):
                y_to = 2 * r_ + k
                mine = (y_to == y) & (kd == k)
                start = kd * HALF + piece * PIECE
                src = emb.at[r_, pl.ds(start, PIECE), :]
                dst = xb.at[x, pl.ds(start, PIECE), pl.ds(pl.multiple_of(y * 256, 256), 256)]
                push(src, dst, sem_a.at[piece, y], dev(x, y_to, z, kd), jnp.logical_not(mine))
                here(src, dst, sem_a.at[piece, y], mine)

    w_rows = pl.ds(pl.multiple_of(z * 1024 + k * 512, 512), 512)
    for step in (1, 3, 2):
        push(
            w_own.at[w_rows, :],
            wb.at[y % 2, w_rows, :],
            sem_w.at[y % 2, k],
            dev(x, rel(y, step), z, y // 2),
        )
    w_local = pltpu.make_async_copy(w_own, wb.at[y % 2], local_sem.at[0])
    pl.when(k == y // 2)(w_local.start)

    o_rows = pl.multiple_of(z * 256 + k * 128, 128)
    for step in (1, 3, 2):
        x_to = rel(x, step)
        push(
            w_out.at[pl.ds(pl.multiple_of(x_to * 1024 + o_rows, 128), 128), :],
            wo.at[y, pl.ds(o_rows, 128), pl.ds(pl.multiple_of(x * 256, 256), 256)],
            sem_wo.at[x],
            dev(x_to, y, z, k),
        )
    o_local = pltpu.make_async_copy(
        w_out.at[pl.ds(pl.multiple_of(x * 1024 + o_rows, 128), 128), :],
        wo.at[y, pl.ds(o_rows, 128), pl.ds(pl.multiple_of(x * 256, 256), 256)],
        local_sem.at[1],
    )
    o_local.start()

    def rows_of(block, core, piece, half=None):
        if half is None:
            return xb.at[block, pl.ds(core * HALF + piece * PIECE, PIECE), :]
        return xb.at[
            block, pl.ds(core * HALF + piece * PIECE + half * (PIECE // 2), PIECE // 2), :
        ]

    xl, xr, xo = rel(x, 3), rel(x, 1), rel(x, 2)
    for piece in range(PIECES):
        for y_ in range(4):
            arrived(
                xb.at[x, pl.ds(k_half + piece * PIECE, PIECE), pl.ds(y_ * 256, 256)],
                sem_a.at[piece, y_],
            )
        block = rows_of(x, k, piece)
        push(block, block, sem_ring.at[0, piece], x_next)
        push(block, block, sem_ring.at[1, piece], x_prev)
        push(block, block, sem_sib.at[0, piece], sib)

    foreign = [(2 * k + j) != y for j in (0, 1)]

    def w_part(j, plane, part):
        return wb.at[j, pl.ds(pl.multiple_of(plane * 1024 + part * 512, 512), 512), :]

    zl, zr, zo = rel(z, 3), rel(z, 1), rel(z, 2)
    for j in (0, 1):
        for part in (0, 1):
            block = w_part(j, z, part)

            @pl.when(foreign[j])
            def _(block=block, j=j, part=part):
                arrived(block, sem_w.at[j, part])

            push(block, block, sem_wz.at[0, j, part], z_next, foreign[j])
            push(block, block, sem_wz.at[1, j, part], z_prev, foreign[j])

    for x_ in (1, 2, 3):
        src_x = rel(x, x_)
        arrived(
            wo.at[y, pl.ds(o_rows, 128), pl.ds(pl.multiple_of(src_x * 256, 256), 256)],
            sem_wo.at[src_x],
        )
    o_local.wait()
    block = wo.at[y, pl.ds(o_rows, 128), :]
    for step in (1, 3, 2):
        push(block, block, sem_wo.at[4 + y], dev(x, rel(y, step), z, k))

    for piece in range(PIECES):
        block = rows_of(xl, k, piece)
        arrived(block, sem_ring.at[0, piece])
        half = rows_of(xl, k, piece, 0)
        push(half, half, sem_ring.at[2, piece], x_next)
        push(block, block, sem_sib.at[1, piece], sib)
        block = rows_of(xr, k, piece)
        arrived(block, sem_ring.at[1, piece])
        half = rows_of(xr, k, piece, 1)
        push(half, half, sem_ring.at[3, piece], x_prev)
        push(block, block, sem_sib.at[2, piece], sib)

    for j in (0, 1):
        for part in (0, 1):
            from_left, from_right = w_part(j, zl, part), w_part(j, zr, part)

            @pl.when(foreign[j])
            def _(from_left=from_left, from_right=from_right, j=j, part=part):
                arrived(from_left, sem_wz.at[0, j, part])
                arrived(from_right, sem_wz.at[1, j, part])

            if part == 0:
                push(from_left, from_left, sem_wz.at[2, j, 0], z_next, foreign[j])
            else:
                push(from_right, from_right, sem_wz.at[2, j, 1], z_prev, foreign[j])

    for piece in range(PIECES):
        block = rows_of(xo, k, piece)
        for half in (0, 1):
            arrived(rows_of(xo, k, piece, half), sem_ring.at[2 + half, piece])
        push(block, block, sem_sib.at[3, piece], sib)

    for step in (1, 2, 3):
        y_ = rel(y, step)
        arrived(wo.at[y_, pl.ds(o_rows, 128), :], sem_wo.at[4 + y_])

    def o_part(plane, core, half=None):
        if half is None:
            return wo.at[:, pl.ds(pl.multiple_of(plane * 256 + core * 128, 128), 128), :]
        return wo.at[:, pl.ds(pl.multiple_of(plane * 256 + core * 128 + half * 64, 64), 64), :]

    for index, block_x in enumerate((x, xl, xr, xo)):
        for piece in range(PIECES):
            arrived(rows_of(block_x, 1 - k, piece), sem_sib.at[index, piece])
    pl.when(k == y // 2)(w_local.wait)
    for j in (0, 1):
        for part in (0, 1):
            block = w_part(j, zo, part)

            @pl.when(foreign[j])
            def _(block=block, j=j, part=part):
                arrived(block, sem_wz.at[2, j, part])

    block = o_part(z, k)
    push(block, block, sem_woz.at[0], z_next)
    push(block, block, sem_woz.at[1], z_prev)
    push(block, block, sem_woz.at[4], sib)

    tile = 256

    def project(step, carry):
        rows = pl.ds(pl.multiple_of(step * tile, tile), tile)
        squares = jnp.zeros((tile, 1), F32)
        accs = [jnp.zeros((tile, 512), F32), jnp.zeros((tile, 512), F32)]
        gate = jnp.zeros((tile, 128), F32)
        for block in range(4):
            a = xb[block, rows, :]
            wide = a.astype(F32)
            squares += jnp.sum(wide * wide, axis=1, keepdims=True)
            depth = slice(block * 1024, block * 1024 + 1024)
            for j in (0, 1):
                accs[j] = accs[j] + dot(a, wb[j, depth, :])
            gate = gate + dot(a, w_gate[depth, :])
        scale = lax.rsqrt(squares / WIDTH + epsilon)
        qk = (accs[0] * scale).astype(BF16)
        qs[rows, :] = qk[:, :KEY]
        ks[rows, :] = qk[:, KEY:]
        vs[rows, :] = (accs[1] * scale).astype(BF16)
        gs[rows, :] = gate * scale + bias[0:1, :]
        return carry

    lax.fori_loop(0, ROWS // tile, project, 0)

    head = 2 * x + k
    gates_t = gs[...].T
    sub = lax.broadcasted_iota(jnp.int32, (128, ROWS), 0)
    gate_in = jnp.sum(jnp.where(sub == head, gates_t, 0.0), axis=0, keepdims=True)
    pre_forget = jnp.sum(jnp.where(sub == head + 8, gates_t, 0.0), axis=0, keepdims=True)
    gate_in = jnp.broadcast_to(gate_in, (8, ROWS))
    pre_forget = jnp.broadcast_to(pre_forget, (8, ROWS))
    log_forget = jnp.minimum(pre_forget, 0.0) - jnp.log1p(jnp.exp(-jnp.abs(pre_forget)))
    lane = lax.broadcasted_iota(jnp.int32, (8, ROWS), 1)
    cum = log_forget
    step = 1
    while step < ROWS:
        cum = cum + jnp.where(lane >= step, pltpu.roll(cum, step, 1), 0.0)
        step *= 2
    lead = gate_in - cum
    peak = lead
    step = 1
    while step < ROWS:
        peak = jnp.maximum(peak, jnp.where(lane >= step, pltpu.roll(peak, step, 1), very_negative))
        step *= 2
    rows_in[0:8, :] = cum
    rows_in[8:16, :] = lead
    rows_in[16:24, :] = peak
    last_peak = jnp.max(lead, axis=1, keepdims=True)[0:1, :]
    decay = jnp.sum(jnp.where(lane == ROWS - 1, cum, 0.0), axis=1, keepdims=True)[0:1, :]
    rows_in[24:32, :] = jnp.exp(lead - last_peak)
    rows_in[32:, :] = jnp.zeros((96, ROWS), F32)
    cols_in[...] = rows_in[...].T

    scaled = ks[...].astype(F32) * cols_in[:, 24:25]
    norm_sum = jnp.sum(scaled, axis=0, keepdims=True)
    memory = lax.dot_general(
        scaled.astype(BF16), vs[...], (((0,), (0,)), ((), ())), preferred_element_type=F32
    )
    chunk = 2 * z + par
    sum_c[chunk] = memory.astype(BF16)
    row = lax.broadcasted_iota(jnp.int32, (8, KEY), 0)
    aux = jnp.where(row == 0, norm_sum, jnp.where(row == 1, decay + last_peak, decay))
    sum_aux[chunk] = aux
    peers = [dev(x, y_mate, z, k)]
    chunks = [2 * z + 1 - par]
    for step in (1, 3, 2):
        peers += [dev(x, y, rel(z, step), k), dev(x, y_mate, rel(z, step), k)]
        chunks += [2 * rel(z, step) + par, 2 * rel(z, step) + 1 - par]
    for peer in peers:
        push(sum_aux.at[chunk], sum_aux.at[chunk], sem_state.at[0, chunk], peer)
        push(sum_c.at[chunk], sum_c.at[chunk], sem_state.at[1, chunk], peer)

    lead_row = rows_in[8:9, :]
    for index in range(ROWS // tile):
        rows = slice(index * tile, (index + 1) * tile)
        seen = (index + 1) * tile
        scores = lax.dot_general(
            qs[rows, :], ks[:seen, :], (((1,), (1,)), ((), ())), preferred_element_type=F32
        )
        t_at = lax.broadcasted_iota(jnp.int32, (tile, seen), 0) + index * tile
        s_at = lax.broadcasted_iota(jnp.int32, (tile, seen), 1)
        exponent = jnp.where(t_at >= s_at, lead_row[:, :seen] - cols_in[rows, 16:17], very_negative)
        weighted = jnp.exp(exponent) * (scores * 0.0625)
        num[rows, :] = dot(weighted.astype(BF16), vs[:seen, :])
        den[rows, :] = jnp.broadcast_to(jnp.sum(weighted, axis=1, keepdims=True), (tile, 128))

    block = o_part(zl, k)
    arrived(block, sem_woz.at[0])
    half = o_part(zl, k, 0)
    push(half, half, sem_woz.at[2], z_next)
    push(block, block, sem_woz.at[5], sib)
    block = o_part(zr, k)
    arrived(block, sem_woz.at[1])
    half = o_part(zr, k, 1)
    push(half, half, sem_woz.at[3], z_prev)
    push(block, block, sem_woz.at[6], sib)

    for chunk_ in chunks:
        arrived(sum_aux.at[chunk_], sem_state.at[0, chunk_])
        arrived(sum_c.at[chunk_], sem_state.at[1, chunk_])

    def combined(limit):
        state_c[...] = jnp.zeros_like(state_c)

        def body(at, state):
            top, norm = state
            here_ = sum_aux[at]
            peak_, decay_ = here_[1:2, :], here_[2:3, :]
            joined = jnp.maximum(decay_ + top, peak_)
            one, two = jnp.exp(decay_ + top - joined), jnp.exp(peak_ - joined)
            state_c[...] = (
                jnp.concatenate([one, one], axis=1) * state_c[...]
                + jnp.concatenate([two, two], axis=1) * sum_c[at].astype(F32)
            )
            return joined, one * norm + two * here_[0:1, :]

        return lax.fori_loop(
            0,
            limit,
            body,
            (jnp.full((1, KEY), very_negative, F32), jnp.zeros((1, KEY), F32)),
        )

    top_in, norm_in = combined(chunk)
    hn_gain = gain[pl.ds(head, 1), :]
    memory_in = state_c[...].astype(BF16)
    for index in range(ROWS // tile):
        rows = slice(index * tile, (index + 1) * tile)
        q = qs[rows, :]
        carried = dot(q, memory_in) * 0.0625
        carried_norm = jnp.sum(q.astype(F32) * norm_in, axis=1, keepdims=True) * 0.0625
        here_max = cols_in[rows, 16:17]
        both = jnp.maximum(top_in[:, 0:1], here_max)
        inner, outer = jnp.exp(here_max - both), jnp.exp(top_in[:, 0:1] - both)
        row_max = cols_in[rows, 0:1] + both
        bottom = inner * den[rows, 0:1] + outer * carried_norm
        divisor = jnp.maximum(jnp.abs(bottom), jnp.exp(-row_max))
        hidden = (inner * num[rows, :] + outer * carried) / divisor
        scale = lax.rsqrt(jnp.mean(hidden * hidden, axis=1, keepdims=True) + epsilon)
        hn[rows, :] = (hidden * scale * hn_gain).astype(BF16)

    other = pl.ds(pl.multiple_of((1 - k) * HALF, HALF), HALF)
    mine_rows = pl.ds(pl.multiple_of(k_half, HALF), HALF)
    push(hn.at[other, :], act.at[k], sem_hn.at[0], sib)
    act[k] = hn[mine_rows, :]
    block = o_part(zo, k)
    arrived(o_part(zo, k, 0), sem_woz.at[2])
    arrived(o_part(zo, k, 1), sem_woz.at[3])
    push(block, block, sem_woz.at[7], sib)
    arrived(act.at[1 - k], sem_hn.at[0])
    for index, plane in enumerate((z, zl, zr, zo)):
        arrived(o_part(plane, 1 - k), sem_woz.at[4 + index])

    def partial(block_x, y_, rows):
        cols = pl.ds(pl.multiple_of(block_x * 256, 256), 256)
        return dot(act[0, rows, :], wo[y_, 0:512, cols]) + dot(
            act[1, rows, :], wo[y_, 512:1024, cols]
        )

    low, high = slice(0, HALF // 2), slice(HALF // 2, HALF)

    def fill(target, block_x, rows, extra=None):
        for y_ in range(4):
            cols = slice(y_ * 256, y_ * 256 + 256)
            value = partial(block_x, y_, rows)
            if extra is not None:
                value = value + extra[:, cols].astype(F32)
            target[rows, cols] = value.astype(target.dtype)

    fill(opp, xo, low)
    push(opp.at[low, :], opp_in.at[0], sem_red.at[0], x_next)
    fill(opp, xo, high)
    push(opp.at[high, :], opp_in.at[1], sem_red.at[1], x_prev)
    fill(right_p, xr, high)
    push(right_p.at[high, :], left_in.at[high, :], sem_red.at[2], x_next)
    fill(left_p, xl, low)
    push(left_p.at[low, :], right_in.at[low, :], sem_red.at[3], x_prev)
    arrived(opp_in.at[0], sem_red.at[0])
    fill(right_p, xr, low, opp_in.at[0])
    push(right_p.at[low, :], left_in.at[low, :], sem_red.at[4], x_next)
    arrived(opp_in.at[1], sem_red.at[1])
    fill(left_p, xl, high, opp_in.at[1])
    push(left_p.at[high, :], right_in.at[high, :], sem_red.at[5], x_prev)
    fill(own_p, x, low)
    fill(own_p, x, high)

    top_end, norm_end = combined(8)
    row = lax.broadcasted_iota(jnp.int32, (8, KEY), 0)
    aux_out[...] = jnp.where(row == 0, norm_end, top_end)
    keep_here = (k == req) & (par == k)
    mem_to = dev(x, 2 * k + req, z, par)
    push(state_c, out_mem, sem_mem.at[0], mem_to, jnp.logical_not(keep_here))
    push(aux_out, out_aux, sem_mem.at[1], mem_to, jnp.logical_not(keep_here))
    here(state_c, out_mem, sem_mem.at[0], keep_here)
    here(aux_out, out_aux, sem_mem.at[1], keep_here)

    for index, rows, sems in ((1, high, (2, 5)), (0, low, (4, 3))):
        arrived(left_in.at[rows, :], sem_red.at[sems[0]])
        arrived(right_in.at[rows, :], sem_red.at[sems[1]])
        total[rows, :] = (
            own_p[rows, :] + left_in[rows, :].astype(F32) + right_in[rows, :].astype(F32)
        ).astype(BF16)
        for y_ in range(4):
            src = total.at[rows, pl.ds(y_ * 256, 256)]
            dst = out_rows.at[
                req, pl.ds(pl.multiple_of(k_half + index * 256, 256), 256), :
            ]
            mine = (y == y_) & (par == k)
            push(
                src, dst, sem_out.at[index, req, k], dev(x, y_, z, par), jnp.logical_not(mine)
            )
            here(src, dst, sem_out.at[index, req, k], mine)

    for index in (1, 0):
        for r_ in (0, 1):
            for k_ in (0, 1):
                arrived(
                    out_rows.at[r_, pl.ds(k_ * HALF + index * 256, 256), :],
                    sem_out.at[index, r_, k_],
                )
    arrived(out_mem, sem_mem.at[0])
    arrived(out_aux, sem_mem.at[1])
    for copy, when in pending:
        if when is None:
            copy.wait_send()
        else:
            pl.when(when)(copy.wait_send)


def local(token_ids, embed_table, norm_gain, w_qkv, w_gate, gate_bias, head_gain, w_out, owner):
    hr_index = lax.axis_index("hr")
    ctx_index = lax.axis_index("ctx")
    embedded = embed_table.at[token_ids].get(mode="promise_in_bounds")
    gain = norm_gain.astype(F32)[:, None]
    w_own = (w_qkv.reshape(WIDTH, 512).astype(F32) * gain).astype(BF16)
    gates = (w_gate.reshape(WIDTH, 16).astype(F32) * gain).astype(BF16)
    gates = jnp.pad(gates, ((0, 0), (0, 112)))
    bias = jnp.broadcast_to(jnp.pad(gate_bias.reshape(1, 16), ((0, 0), (0, 112))), (8, 128))
    vmem = pl.BlockSpec(memory_space=pltpu.VMEM)
    hbm = pl.BlockSpec(memory_space=pl.ANY)
    dma = pltpu.SemaphoreType.DMA
    rows, mem, aux = pl.pallas_call(
        kernel,
        out_shape=(
            jax.ShapeDtypeStruct((2, ROWS, 256), BF16),
            jax.ShapeDtypeStruct((KEY, VAL), F32),
            jax.ShapeDtypeStruct((8, KEY), F32),
        ),
        in_specs=[vmem, hbm, hbm, vmem, vmem, vmem],
        out_specs=(vmem, vmem, vmem),
        scratch_shapes=[
            pltpu.VMEM((4, ROWS, 1024), BF16),
            pltpu.VMEM((2, WIDTH, 512), BF16),
            pltpu.VMEM((4, 1024, 1024), BF16),
            pltpu.VMEM((ROWS, KEY), BF16),
            pltpu.VMEM((ROWS, KEY), BF16),
            pltpu.VMEM((ROWS, VAL), BF16),
            pltpu.VMEM((ROWS, 128), F32),
            pltpu.VMEM((ROWS, VAL), F32),
            pltpu.VMEM((ROWS, 128), F32),
            pltpu.VMEM((128, ROWS), F32),
            pltpu.VMEM((ROWS, 128), F32),
            pltpu.VMEM((8, KEY, VAL), BF16),
            pltpu.VMEM((8, 8, KEY), F32),
            pltpu.VMEM((KEY, VAL), F32),
            pltpu.VMEM((ROWS, VAL), BF16),
            pltpu.VMEM((2, HALF, VAL), BF16),
            pltpu.VMEM((HALF, 1024), BF16),
            pltpu.VMEM((HALF, 1024), BF16),
            pltpu.VMEM((HALF, 1024), BF16),
            pltpu.VMEM((HALF, 1024), F32),
            pltpu.VMEM((2, HALF // 2, 1024), BF16),
            pltpu.VMEM((HALF, 1024), BF16),
            pltpu.VMEM((HALF, 1024), BF16),
            pltpu.VMEM((HALF, 1024), BF16),
            pltpu.VMEM((8, KEY), F32),
            pltpu.VMEM((8, KEY), F32),
            dma((SENDS,)),
            dma((2,)),
            dma((PIECES, 4)),
            dma((4, PIECES)),
            dma((4, PIECES)),
            dma((2, 2)),
            dma((3, 2, 2)),
            dma((8,)),
            dma((8,)),
            dma((2, 8)),
            dma((1,)),
            dma((6,)),
            dma((2, 2, 2)),
            dma((2,)),
        ],
        compiler_params=pltpu.CompilerParams(
            collective_id=0, has_side_effects=True, vmem_limit_bytes=60 * 2**20
        ),
    )(embedded, w_own, w_out, gates, bias, head_gain.astype(F32))
    block_out = (embedded.astype(F32) + rows.astype(F32)).astype(BF16)
    owner_here = lax.dynamic_slice_in_dim(owner, hr_index, 1, 0)[0]
    keep = (owner_here == ctx_index).astype(F32)
    memory_c = (keep * mem)[None, None, None]
    memory_n = (keep * aux[0])[None, None, None]
    memory_m = (keep * aux[1, 0:1])[None, None]
    return (block_out, memory_c, memory_n, memory_m)


def solution(mesh):
    return jax.shard_map(
        local,
        mesh=mesh,
        in_specs=(
            P(None, "ctx"),
            P(None, "hr"),
            P(),
            P(None, "hr", None, None),
            P(),
            P(),
            P(),
            P(None, "hr"),
            P(),
        ),
        out_specs=(
            P(None, "ctx", "hr"),
            P("ctx", "hr", None, None, None),
            P("ctx", "hr", None, None),
            P("ctx", "hr", None),
        ),
        check_vma=False,
    )
```

time: 559 us -> 234 us (0.42)
  waiting for transfers between devices: 293 us -> 0 us
  Pallas kernels: 0 us -> 192 us
  starting transfers between devices: 84.2 us -> 0 us
  blocking collectives: 54.8 us -> 0 us
  matrix products: 44.7 us -> 0 us
  between operations: 21.8 us -> 3.12 us
  other arithmetic: 27.3 us -> 12.3 us
    all_gather x2 -> x0, waiting for transfers between devices: 232 us -> none  [the longest x1 122 us: local(): piece = lax.all_gather(normed_local, 'hr', axis=2, tiled=True)]
    pallas_call x0 -> x1, Pallas kernels: none -> 192 us  [local(): pl.pallas_call(kernel, out_shape=(jax.ShapeDtypeStruct((2, ROWS, 256), BF...]
    ppermute x22 -> x0, starting transfers between devices: 84.1 us -> none  [the longest x21 83.2 us: passed_along(): lax.ppermute(value, axis, [(source, source + steps) for source in range(l...]
    psum x2 -> x0, blocking collectives: 54.8 us -> none  [the longest x1 37 us: local(): square_sums = lax.psum(jnp.sum(wide_local * wide_local, axis=2), 'hr')]
    dot_general x10 -> x0, matrix products: 44.7 us -> none  [the longest x1 10.3 us: local(): jnp.einsum('rtc,cn->rtn', piece, gate_flat, preferred_element_type=jnp.fl...]
    psum x1 -> x0, waiting for transfers between devices: 37.9 us -> none  [from_root(): return lax.psum(jnp.where(mine, value, jnp.zeros_like(value)), axis)]
    ppermute x22 -> x0, waiting for transfers between devices: 22.8 us -> none  [the longest x1 21.8 us: swapped(): return lax.ppermute(value, axis, pairs)]
  transfers between devices with their start and end apart: 25 -> 0, of which waited for: 6 -> 0; matrix products, arithmetic and copies ran while one was open for 3% -> 0% of each run, Pallas kernels for 0% -> 0%
where the time goes in v1:
time: 234 us; the launch traced here: 230 us
  Pallas kernels  192 us (82%)
  local copies, waits for them, and re-layouts  22.7 us (10%)
  other arithmetic  12.3 us (5%)
  between operations  3.12 us (1%)
    pallas_call x1, Pallas kernels, local(): pl.pallas_call(kernel, out_shape=(jax.ShapeDtypeStruct((2, ROWS, 256), BF...  192 us
    gather x1, local copies, waits for them, and re-layouts, local(): embedded = embed_table.at[token_ids].get(mode='promise_in_bounds')  16.4 us

profile of v1, /device:TPU:8, one launch (start us, length us, event | category | flops | bytes accessed | tf_op | source)
XLA Modules:
  0.0 230.5 jit_solution(7939499662862436684)
XLA Ops:
  0.6 1.2 dynamic_slice.3
  2.5 0.8 reshape.30
  3.3 0.6 broadcast_in_dim.20.bias
  3.9 0.7 fusion.1
  4.6 0.7 convert_element_type.43
  5.3 1.3 convert_element_type.48.gain
  6.6 0.9 bitcast_convert_fusion
  7.5 16.4 %gather_fusion = bf16[2048,256]{1,0:T(8,128)(2,1)} fusion(bf16[32768,256]{1,0:T(8,128)(2,1)} %param.10, s32[2048]{0:T(1024)S(1)} %bitcast_clamp_fusion), kind=kCustom, calls=%fused_computation | custom fusion | bytes 2105344 | tf_op jit(solution)/shard_map/gather | solution.py:518
  24.0 0.6 copy.15
  24.6 0.0 copy-start.1
  24.6 0.7 multiply_convert_fusion
  25.3 1.2 pad.8.w_gate
  26.5 0.7 copy-done.1
  27.1 2.4 %fusion.w_own = bf16[4096,512]{1,0:T(8,128)(2,1)} fusion(bf16[4096,1,1,512]{3,0,2,1:T(8,128)(2,1)S(1)} %copy-done.1, f32[4096]{0:T(1024)S(1)} %convert_element_type.43), kind=kLoop, calls=%fused_computation.2 | loop fusion | flops 6291456 | bytes 8404992 | tf_op jit(solution)/shard_map/convert_element_type | solution.py:520
  29.5 0.0 copy-start
  29.5 192.4 %shard_map.120 = (bf16[2,1024,256]{2,1,0:T(8,128)(2,1)}, f32[256,512]{1,0:T(8,128)}, f32[8,256]{1,0:T(8,128)}) custom-call(bf16[2,1024,256]{2,1,0:T(8,128)(2,1)} %bitcast.21, bf16[4096,512]{1,0:T(8,128)(2,1)} %fusion.w_own, bf16[4096,256]{1,0:T(8,128)(2,1)} %w_out.1, bf16[4096,128]{1,0:T(8,128)(2,1)} %pad.8.w_gate, f32[8,128]{1,0:T(8,128)} %broadcast_in_dim.20.bias, ...), custom_call_target="tpu_custom_call" | custom-call | tf_op jit(solution)/shard_map/pallas_call | solution.py:527
  221.9 1.2 slice.7
  223.8 0.0 copy-done
  223.8 2.5 %add_convert_fusion = bf16[2,1024,256]{2,1,0:T(8,128)(2,1)} fusion(bf16[2,1024,256]{2,1,0:T(8,128)(2,1)} %get-tuple-element.7, bf16[2,1024,256]{2,1,0:T(8,128)(2,1)S(1)} %bitcast.22), kind=kLoop, calls=%fused_computation.3 | loop fusion | flops 2097152 | bytes 3145728 | tf_op jit(solution)/shard_map/convert_element_type | solution.py:582
  226.2 1.3 multiply_bitcast_fusion.1
  227.5 1.9 multiply_bitcast_fusion
  (2 shorter events, 0.0 us)
Async XLA Ops:
  24.6 2.6 %copy-start.1 = (bf16[4096,1,1,512]{3,0,2,1:T(8,128)(2,1)S(1)}, bf16[4096,1,1,512]{3,0,2,1:T(8,128)(2,1)}, u32[]{:S(2)}) copy-start(bf16[4096,1,1,512]{3,0,2,1:T(8,128)(2,1)} %param.12) | copy-start | bytes 12582916
  29.5 194.2 %copy-start = (bf16[2048,256]{1,0:T(8,128)(2,1)S(1)}, bf16[2048,256]{1,0:T(8,128)(2,1)}, u32[]{:S(2)}) copy-start(bf16[2048,256]{1,0:T(8,128)(2,1)} %gather_fusion) | copy-start | bytes 3145732

commit v2 on v1

v2 whole, which is shorter than its diff:
```python
import jax
import jax.numpy as jnp
from jax import lax
from jax.experimental import pallas as pl
from jax.experimental.pallas import tpu as pltpu
from jax.sharding import PartitionSpec as P

MESH = pl.DeviceIdType.MESH
F32 = jnp.float32
BF16 = jnp.bfloat16
very_negative = -1e30
epsilon = 1e-06

WIDTH = 4096
ROWS = 1024
HALF = 512
PIECES = 2
PIECE = HALF // PIECES
KEY = 256
VAL = 512
SENDS = 128
SPREAD = 320
DIRECT = 768
TILE = 256


def dot(a, b):
    return jnp.dot(a, b, preferred_element_type=F32)


def dot_t(a, b):
    return lax.dot_general(a, b, (((1,), (1,)), ((), ())), preferred_element_type=F32)


def kernel(
    emb,
    w_own,
    w_out,
    w_gate,
    norm_gain,
    head_gain,
    bias,
    owner,
    out,
    out_mem,
    out_aux,
    xb,
    wb,
    wo,
    qs,
    ks,
    vs,
    gs,
    num,
    den,
    rows_in,
    cols_in,
    sum_c,
    sum_aux,
    pair_c,
    pair_aux,
    state_c,
    hn,
    act,
    own_p,
    total,
    rows_got,
    mem_got,
    aux_got,
    aux_out,
    send_sem,
    local_sem,
    sem_a,
    sem_ring,
    sem_sib,
    sem_w,
    sem_wz,
    sem_wo,
    sem_woz,
    sem_wos,
    sem_mate,
    sem_pair,
    sem_hn,
    sem_act,
    sem_out,
    sem_mem,
):
    c = lax.axis_index("ctx")
    h = lax.axis_index("hr")
    x, y = h // 4, h % 4
    z, k = c // 2, c % 2
    req, par = y // 2, y % 2

    def dev(x_, y_, z_, k_):
        return (z_ * 2 + k_, x_ * 4 + y_)

    def rel(base, step):
        return lax.rem(base + step, 4)

    sib = dev(x, y, z, 1 - k)
    x_next, x_prev = dev(rel(x, 1), y, z, k), dev(rel(x, 3), y, z, k)
    y_next, y_prev = dev(x, rel(y, 1), z, k), dev(x, rel(y, 3), z, k)
    z_next, z_prev = dev(x, y, rel(z, 1), k), dev(x, y, rel(z, 3), k)
    mate = dev(x, 2 * req + 1 - par, z, k)

    partners = [sib]
    for step in (1, 2, 3):
        for core in (0, 1):
            partners.append(dev(x, rel(y, step), z, core))
        partners.append(dev(rel(x, step), y, z, k))
        partners.append(dev(x, y, rel(z, step), k))
    barrier = pltpu.get_barrier_semaphore()
    for partner in partners:
        pl.semaphore_signal(barrier, inc=1, device_id=partner, device_id_type=MESH)
    pl.semaphore_wait(barrier, len(partners))

    pending = []

    def push(src, dst, sem, target, when=None):
        slot = len(pending)
        copy = pltpu.make_async_remote_copy(
            src_ref=src,
            dst_ref=dst,
            send_sem=send_sem.at[slot],
            recv_sem=sem,
            device_id=target,
            device_id_type=MESH,
        )
        pending.append((copy, when))
        if when is None:
            copy.start()
        else:
            pl.when(when)(copy.start)

    def here(src, dst, sem, when):
        copy = pltpu.make_async_copy(src, dst, sem)
        pl.when(when)(copy.start)

    def arrived(dst, sem, when=None):
        copy = pltpu.make_async_remote_copy(
            src_ref=dst,
            dst_ref=dst,
            send_sem=send_sem.at[0],
            recv_sem=sem,
            device_id=sib,
            device_id_type=MESH,
        )
        if when is None:
            copy.wait_recv()
        else:
            pl.when(when)(copy.wait_recv)

    k_half = k * HALF
    xl, xr, xo = rel(x, 3), rel(x, 1), rel(x, 2)
    zl, zr, zo = rel(z, 3), rel(z, 1), rel(z, 2)

    for piece in range(PIECES):
        for r_ in (0, 1):
            for kd in (0, 1):
                y_to = 2 * r_ + k
                mine = (y_to == y) & (kd == k)
                start = kd * HALF + piece * PIECE
                src = emb.at[r_, pl.ds(start, PIECE), :]
                dst = xb.at[x, pl.ds(start, PIECE), pl.ds(pl.multiple_of(y * 256, 256), 256)]
                push(src, dst, sem_a.at[piece, y], dev(x, y_to, z, kd), jnp.logical_not(mine))
                here(src, dst, sem_a.at[piece, y], mine)

    w_local = pltpu.make_async_copy(w_own, wb.at[y % 2], local_sem.at[0])
    pl.when(k == y // 2)(w_local.start)
    o_local = pltpu.make_async_copy(w_out, wo.at[y], local_sem.at[1])
    o_local.start()

    def rows_of(block, core, piece, half=None):
        start, size = core * HALF + piece * PIECE, PIECE
        if half is not None:
            start, size = start + half * (PIECE // 2), PIECE // 2
        return xb.at[block, pl.ds(start, size), :]

    def ring_start(piece):
        for y_ in range(4):
            arrived(
                xb.at[x, pl.ds(k_half + piece * PIECE, PIECE), pl.ds(y_ * 256, 256)],
                sem_a.at[piece, y_],
            )
        block = rows_of(x, k, piece)
        push(block, block, sem_ring.at[0, piece], x_next)
        push(block, block, sem_ring.at[1, piece], x_prev)
        push(block, block, sem_sib.at[0, piece], sib)

    def ring_middle(piece):
        block = rows_of(xl, k, piece)
        arrived(block, sem_ring.at[0, piece])
        half = rows_of(xl, k, piece, 0)
        push(half, half, sem_ring.at[2, piece], x_next)
        push(block, block, sem_sib.at[1, piece], sib)
        block = rows_of(xr, k, piece)
        arrived(block, sem_ring.at[1, piece])
        half = rows_of(xr, k, piece, 1)
        push(half, half, sem_ring.at[3, piece], x_prev)
        push(block, block, sem_sib.at[2, piece], sib)

    def ring_end(piece):
        for half in (0, 1):
            arrived(rows_of(xo, k, piece, half), sem_ring.at[2 + half, piece])
        block = rows_of(xo, k, piece)
        push(block, block, sem_sib.at[3, piece], sib)

    def w_part(kind, j, plane, part, half=None):
        if kind == 0:
            start, size = (plane * 2 + part) * SPREAD, SPREAD
        else:
            start, size = 8 * SPREAD + part * DIRECT, DIRECT
        if half is not None:
            start, size = start + half * (size // 2), size // 2
        if not isinstance(start, int):
            start = pl.multiple_of(start, 32)
        return (j, pl.ds(start, size), slice(None))

    def w_send(kind):
        at = w_part(kind, y % 2, z, k)
        src = w_own.at[at[1], at[2]]
        core = y // 2
        push(src, wb.at[at], sem_w.at[kind, y % 2, k, 0], dev(x, rel(y, 1), z, core))
        push(src, wb.at[at], sem_w.at[kind, y % 2, k, 0], dev(x, rel(y, 3), z, core))

    away = [lax.rem(y - 2 * k - j + 4, 4) for j in (0, 1)]
    foreign = [step != 0 for step in away]

    def w_near(kind):
        for j in (0, 1):
            near = (away[j] == 1) | (away[j] == 3)
            for part in (0, 1):
                arrived(wb.at[w_part(kind, j, z, part)], sem_w.at[kind, j, part, 0], near)
                half = wb.at[w_part(kind, j, z, part, 0)]
                push(half, half, sem_w.at[kind, j, part, 0], y_next, away[j] == 1)
                half = wb.at[w_part(kind, j, z, part, 1)]
                push(half, half, sem_w.at[kind, j, part, 1], y_prev, away[j] == 3)

    def w_far(kind):
        for j in (0, 1):
            for part in (0, 1):
                for half in (0, 1):
                    arrived(
                        wb.at[w_part(kind, j, z, part, half)],
                        sem_w.at[kind, j, part, half],
                        away[j] == 2,
                    )

    def w_along_z(distances):
        for j in (0, 1):
            right = away[j] == distances[0]
            for other in distances[1:]:
                right = right | (away[j] == other)
            for part in (0, 1):
                block = wb.at[w_part(0, j, z, part)]
                push(block, block, sem_wz.at[0, j, part], z_next, right)
                push(block, block, sem_wz.at[1, j, part], z_prev, right)

    ring_start(0)
    w_send(0)
    ring_start(1)
    w_near(0)
    w_along_z((1, 3))
    w_send(1)
    ring_middle(0)
    w_far(0)
    w_along_z((2,))
    ring_middle(1)
    w_near(1)

    def o_part(y_, plane, core, half=None):
        start, size = plane * 1024 + core * 512, 512
        if half is not None:
            start, size = start + half * 256, 256
        return wo.at[y_, pl.ds(pl.multiple_of(start, 256), size), :]

    for step in (1, 3, 2):
        push(
            w_out.at[pl.ds(pl.multiple_of(z * 1024 + k * 512, 512), 512), :],
            o_part(y, z, k),
            sem_wo.at[y],
            dev(x, rel(y, step), z, k),
        )

    for j in (0, 1):
        for part in (0, 1):
            from_left, from_right = wb.at[w_part(0, j, zl, part)], wb.at[w_part(0, j, zr, part)]
            arrived(from_left, sem_wz.at[0, j, part], foreign[j])
            arrived(from_right, sem_wz.at[1, j, part], foreign[j])
            if part == 0:
                push(from_left, from_left, sem_wz.at[2, j, 0], z_next, foreign[j])
            else:
                push(from_right, from_right, sem_wz.at[2, j, 1], z_prev, foreign[j])

    ring_end(0)
    ring_end(1)
    w_far(1)
    pl.when(k == y // 2)(w_local.wait)
    for j in (0, 1):
        for part in (0, 1):
            arrived(wb.at[w_part(0, j, zo, part)], sem_wz.at[2, j, part], foreign[j])

    others = [rel(y, step) for step in (1, 2, 3)]
    for index, y_ in enumerate(others):
        block = o_part(y_, z, k)
        arrived(block, sem_wo.at[y_])
        push(block, block, sem_woz.at[0, index], z_next)
        push(block, block, sem_woz.at[1, index], z_prev)
        push(block, block, sem_wos.at[0, index], sib)

    for index, block_x in enumerate((x, xl, xr, xo)):
        for piece in range(PIECES):
            arrived(rows_of(block_x, 1 - k, piece), sem_sib.at[index, piece])

    def project(step, carry):
        rows = pl.ds(pl.multiple_of(step * TILE, TILE), TILE)
        squares = jnp.zeros((TILE, 1), F32)
        for block in range(4):
            wide = xb[block, rows, :].astype(F32)
            squares += jnp.sum(wide * wide, axis=1, keepdims=True)
        scale = lax.rsqrt(squares / WIDTH + epsilon)
        accs = [jnp.zeros((TILE, 512), F32), jnp.zeros((TILE, 512), F32)]
        gate = jnp.zeros((16, TILE), F32)
        for block in range(4):
            depth = slice(block * 1024, block * 1024 + 1024)
            wide = xb[block, rows, :].astype(F32)
            normed = (wide * scale * norm_gain[block : block + 1, :]).astype(BF16)
            for j in (0, 1):
                accs[j] = accs[j] + dot(normed, wb[j, depth, :])
            gate = gate + dot_t(w_gate[:, depth], normed)
        qs[rows, :] = accs[0][:, :KEY].astype(BF16)
        ks[rows, :] = accs[0][:, KEY:].astype(BF16)
        vs[rows, :] = accs[1].astype(BF16)
        gs[:, rows] = gate
        return carry

    lax.fori_loop(0, ROWS // TILE, project, 0)

    head = 2 * x + k
    gates = gs[...]
    sub = lax.broadcasted_iota(jnp.int32, (16, ROWS), 0)
    gate_in = jnp.sum(jnp.where(sub == head, gates, 0.0), axis=0, keepdims=True)
    pre_forget = jnp.sum(jnp.where(sub == head + 8, gates, 0.0), axis=0, keepdims=True)
    gate_in = jnp.broadcast_to(gate_in, (8, ROWS)) + bias[0, head]
    pre_forget = jnp.broadcast_to(pre_forget, (8, ROWS)) + bias[1, head]
    log_forget = jnp.minimum(pre_forget, 0.0) - jnp.log1p(jnp.exp(-jnp.abs(pre_forget)))
    lane = lax.broadcasted_iota(jnp.int32, (8, ROWS), 1)
    cum = log_forget
    step = 1
    while step < ROWS:
        cum = cum + jnp.where(lane >= step, pltpu.roll(cum, step, 1), 0.0)
        step *= 2
    lead = gate_in - cum
    peak = lead
    step = 1
    while step < ROWS:
        peak = jnp.maximum(peak, jnp.where(lane >= step, pltpu.roll(peak, step, 1), very_negative))
        step *= 2
    rows_in[0:8, :] = cum
    rows_in[8:16, :] = lead
    rows_in[16:24, :] = peak
    last_peak = jnp.max(lead, axis=1, keepdims=True)[0:1, :]
    decay = jnp.sum(jnp.where(lane == ROWS - 1, cum, 0.0), axis=1, keepdims=True)[0:1, :]
    rows_in[24:32, :] = jnp.exp(lead - last_peak)
    rows_in[32:, :] = jnp.zeros((96, ROWS), F32)
    cols_in[...] = rows_in[...].T

    scaled = ks[...].astype(F32) * cols_in[:, 24:25]
    norm_sum = jnp.sum(scaled, axis=0, keepdims=True)
    memory = lax.dot_general(
        scaled.astype(BF16), vs[...], (((0,), (0,)), ((), ())), preferred_element_type=F32
    )
    sum_c[par] = memory.astype(BF16)
    row = lax.broadcasted_iota(jnp.int32, (8, KEY), 0)
    sum_aux[par] = jnp.where(row == 0, norm_sum, jnp.where(row == 1, decay + last_peak, decay))
    push(sum_aux.at[par], sum_aux.at[par], sem_mate.at[0], mate)
    push(sum_c.at[par], sum_c.at[par], sem_mate.at[1], mate)

    lead_row = rows_in[8:9, :]

    def within(index):
        rows = slice(index * TILE, (index + 1) * TILE)
        seen = (index + 1) * TILE
        scores = dot_t(qs[rows, :], ks[:seen, :])
        t_at = lax.broadcasted_iota(jnp.int32, (TILE, seen), 0) + index * TILE
        s_at = lax.broadcasted_iota(jnp.int32, (TILE, seen), 1)
        exponent = jnp.where(t_at >= s_at, lead_row[:, :seen] - cols_in[rows, 16:17], very_negative)
        weighted = jnp.exp(exponent) * (scores * 0.0625)
        num[rows, :] = dot(weighted.astype(BF16), vs[:seen, :])
        den[rows, :] = jnp.broadcast_to(jnp.sum(weighted, axis=1, keepdims=True), (TILE, 128))

    def twice(value):
        return jnp.concatenate([value, value], axis=1)

    def join(state, c_ref, aux_ref, at):
        decay_, top, norm = state
        later = aux_ref[at]
        peak_, falls = later[1:2, :], later[2:3, :]
        joined = jnp.maximum(falls + top, peak_)
        one, two = jnp.exp(falls + top - joined), jnp.exp(peak_ - joined)
        state_c[...] = twice(one) * state_c[...] + twice(two) * c_ref[at].astype(F32)
        return decay_ + falls, joined, one * norm + two * later[0:1, :]

    def start_state():
        state_c[...] = jnp.zeros_like(state_c)
        zero = jnp.zeros((1, KEY), F32)
        return zero, jnp.full((1, KEY), very_negative, F32), zero

    for index in (0, 1):
        within(index)
    other = 1 - par
    arrived(sum_aux.at[other], sem_mate.at[0])
    arrived(sum_c.at[other], sem_mate.at[1])
    state = start_state()
    for at in (0, 1):
        state = join(state, sum_c, sum_aux, at)
    pair_c[z] = state_c[...].astype(BF16)
    pair_aux[z] = jnp.where(row == 0, state[2], jnp.where(row == 1, state[1], state[0]))
    for step in (1, 3, 2):
        to = dev(x, y, rel(z, step), k)
        push(pair_aux.at[z], pair_aux.at[z], sem_pair.at[0, z], to)
        push(pair_c.at[z], pair_c.at[z], sem_pair.at[1, z], to)
    for index in (2, 3):
        within(index)

    for step in (1, 3, 2):
        z_ = rel(z, step)
        arrived(pair_aux.at[z_], sem_pair.at[0, z_])
        arrived(pair_c.at[z_], sem_pair.at[1, z_])

    for index, y_ in enumerate(others):
        from_left, from_right = o_part(y_, zl, k), o_part(y_, zr, k)
        arrived(from_left, sem_woz.at[0, index])
        arrived(from_right, sem_woz.at[1, index])
        half = o_part(y_, zl, k, 0)
        push(half, half, sem_woz.at[2, index], z_next)
        half = o_part(y_, zr, k, 1)
        push(half, half, sem_woz.at[3, index], z_prev)

    def pairs(limit):
        return lax.fori_loop(
            0, limit, lambda at, state: join(state, pair_c, pair_aux, at), start_state()
        )

    state = pairs(z)
    _, top_in, norm_in = lax.fori_loop(
        0, par, lambda at, state: join(state, sum_c, sum_aux, at), state
    )
    sub8 = lax.broadcasted_iota(jnp.int32, (8, VAL), 0)
    gain = jnp.sum(
        jnp.where(sub8 == head, head_gain[...].astype(F32), 0.0), axis=0, keepdims=True
    )
    memory_in = state_c[...].astype(BF16)

    def finish(start):
        rows = pl.ds(pl.multiple_of(start, TILE), TILE)
        q = qs[rows, :]
        carried = dot(q, memory_in) * 0.0625
        carried_norm = jnp.sum(q.astype(F32) * norm_in, axis=1, keepdims=True) * 0.0625
        columns = cols_in[rows, :]
        here_max = columns[:, 16:17]
        both = jnp.maximum(top_in[:, 0:1], here_max)
        inner, outer = jnp.exp(here_max - both), jnp.exp(top_in[:, 0:1] - both)
        row_max = columns[:, 0:1] + both
        bottom = inner * den[rows, :][:, 0:1] + outer * carried_norm
        divisor = jnp.maximum(jnp.abs(bottom), jnp.exp(-row_max))
        hidden = (inner * num[rows, :] + outer * carried) / divisor
        scale = lax.rsqrt(jnp.mean(hidden * hidden, axis=1, keepdims=True) + epsilon)
        return (hidden * scale * gain).astype(BF16)

    def act_of(block, kk, tile, half=None):
        start, size = tile * TILE, TILE
        if half is not None:
            start, size = start + half * (TILE // 2), TILE // 2
        return act.at[block, kk, pl.ds(start, size), :]

    def act_start(kk, order, tile):
        block = act_of(x, kk, tile)
        push(block, block, sem_act.at[0, order, tile], x_next)
        push(block, block, sem_act.at[1, order, tile], x_prev)

    for tile in (0, 1):
        act[x, k, tile * TILE : (tile + 1) * TILE, :] = finish(k_half + tile * TILE)
        act_start(k, 0, tile)
    for tile in (0, 1):
        rows = slice(tile * TILE, (tile + 1) * TILE)
        hn[rows, :] = finish((1 - k) * HALF + tile * TILE)
        push(hn.at[rows, :], act_of(x, k, tile), sem_hn.at[tile], sib)
    for tile in (0, 1):
        arrived(act_of(x, 1 - k, tile), sem_hn.at[tile])
        act_start(1 - k, 1, tile)

    for index, y_ in enumerate(others):
        block = o_part(y_, zl, k)
        push(block, block, sem_wos.at[1, index], sib)
        block = o_part(y_, zr, k)
        push(block, block, sem_wos.at[2, index], sib)
        arrived(o_part(y_, zo, k, 0), sem_woz.at[2, index])
        arrived(o_part(y_, zo, k, 1), sem_woz.at[3, index])
        block = o_part(y_, zo, k)
        push(block, block, sem_wos.at[3, index], sib)

    for order, kk in ((0, k), (1, 1 - k)):
        for tile in (0, 1):
            arrived(act_of(xl, kk, tile), sem_act.at[0, order, tile])
            half = act_of(xl, kk, tile, 0)
            push(half, half, sem_act.at[2, order, tile], x_next)
            arrived(act_of(xr, kk, tile), sem_act.at[1, order, tile])
            half = act_of(xr, kk, tile, 1)
            push(half, half, sem_act.at[3, order, tile], x_prev)

    _, top_end, norm_end = pairs(4)
    aux_out[...] = jnp.where(row == 0, norm_end, top_end)
    keep_here = (k == req) & (par == k)
    mem_to = dev(x, 2 * k + req, z, par)
    push(state_c, mem_got, sem_mem.at[0], mem_to, jnp.logical_not(keep_here))
    push(aux_out, aux_got, sem_mem.at[1], mem_to, jnp.logical_not(keep_here))
    here(state_c, mem_got, sem_mem.at[0], keep_here)
    here(aux_out, aux_got, sem_mem.at[1], keep_here)

    o_local.wait()
    for index, y_ in enumerate(others):
        for at, plane in enumerate((z, zl, zr, zo)):
            arrived(o_part(y_, plane, 1 - k), sem_wos.at[at, index])

    def mixed(block, tile, y_):
        rows = slice(tile * TILE, (tile + 1) * TILE)
        start = pl.multiple_of(block * 1024, 1024)
        return dot(act[block, 0, rows, :], wo[y_, pl.ds(start, 512), :]) + dot(
            act[block, 1, rows, :], wo[y_, pl.ds(start + 512, 512), :]
        )

    for tile in (0, 1):
        for y_ in range(4):
            own_p[tile * TILE : (tile + 1) * TILE, y_ * 256 : y_ * 256 + 256] = (
                mixed(x, tile, y_) + mixed(xl, tile, y_) + mixed(xr, tile, y_)
            )
    for tile in (0, 1):
        rows = slice(tile * TILE, (tile + 1) * TILE)
        for order, kk in ((0, k), (1, 1 - k)):
            for half in (0, 1):
                arrived(act_of(xo, kk, tile, half), sem_act.at[2 + half, order, tile])
        for y_ in range(4):
            cols = slice(y_ * 256, y_ * 256 + 256)
            total[rows, cols] = (own_p[rows, cols] + mixed(xo, tile, y_)).astype(BF16)
            src = total.at[rows, cols]
            dst = rows_got.at[req, pl.ds(pl.multiple_of(k_half + tile * TILE, TILE), TILE), :]
            mine = (y == y_) & (par == k)
            push(src, dst, sem_out.at[tile, req, k], dev(x, y_, z, par), jnp.logical_not(mine))
            here(src, dst, sem_out.at[tile, req, k], mine)

    arrived(mem_got, sem_mem.at[0])
    arrived(aux_got, sem_mem.at[1])
    keep = jnp.where(owner[h] == c, 1.0, 0.0)
    out_mem[...] = mem_got[...] * keep
    out_aux[...] = aux_got[...] * keep
    for tile in (0, 1):
        for r_ in (0, 1):
            for k_ in (0, 1):
                rows = slice(k_ * HALF + tile * TILE, k_ * HALF + (tile + 1) * TILE)
                arrived(rows_got.at[r_, rows, :], sem_out.at[tile, r_, k_])
                out[r_, rows, :] = (
                    emb[r_, rows, :].astype(F32) + rows_got[r_, rows, :].astype(F32)
                ).astype(BF16)
    for copy, when in pending:
        if when is None:
            copy.wait_send()
        else:
            pl.when(when)(copy.wait_send)


def local(token_ids, embed_table, norm_gain, w_qkv, w_gate, gate_bias, head_gain, w_out, owner):
    embedded = embed_table.at[token_ids].get(mode="promise_in_bounds")
    gates = jnp.transpose(w_gate, (1, 2, 0)).reshape(16, WIDTH)
    vmem = pl.BlockSpec(memory_space=pltpu.VMEM)
    smem = pl.BlockSpec(memory_space=pltpu.SMEM)
    hbm = pl.BlockSpec(memory_space=pl.ANY)
    dma = pltpu.SemaphoreType.DMA
    block_out, mem, aux = pl.pallas_call(
        kernel,
        out_shape=(
            jax.ShapeDtypeStruct((2, ROWS, 256), BF16),
            jax.ShapeDtypeStruct((KEY, VAL), F32),
            jax.ShapeDtypeStruct((8, KEY), F32),
        ),
        in_specs=[vmem, hbm, hbm, vmem, vmem, vmem, smem, smem],
        out_specs=(vmem, vmem, vmem),
        scratch_shapes=[
            pltpu.VMEM((4, ROWS, 1024), BF16),
            pltpu.VMEM((2, WIDTH, 512), BF16),
            pltpu.VMEM((4, WIDTH, 256), BF16),
            pltpu.VMEM((ROWS, KEY), BF16),
            pltpu.VMEM((ROWS, KEY), BF16),
            pltpu.VMEM((ROWS, VAL), BF16),
            pltpu.VMEM((16, ROWS), F32),
            pltpu.VMEM((ROWS, VAL), F32),
            pltpu.VMEM((ROWS, 128), F32),
            pltpu.VMEM((128, ROWS), F32),
            pltpu.VMEM((ROWS, 128), F32),
            pltpu.VMEM((2, KEY, VAL), BF16),
            pltpu.VMEM((2, 8, KEY), F32),
            pltpu.VMEM((4, KEY, VAL), BF16),
            pltpu.VMEM((4, 8, KEY), F32),
            pltpu.VMEM((KEY, VAL), F32),
            pltpu.VMEM((HALF, VAL), BF16),
            pltpu.VMEM((4, 2, HALF, VAL), BF16),
            pltpu.VMEM((HALF, 1024), F32),
            pltpu.VMEM((HALF, 1024), BF16),
            pltpu.VMEM((2, ROWS, 256), BF16),
            pltpu.VMEM((KEY, VAL), F32),
            pltpu.VMEM((8, KEY), F32),
            pltpu.VMEM((8, KEY), F32),
            dma((SENDS,)),
            dma((2,)),
            dma((PIECES, 4)),
            dma((4, PIECES)),
            dma((4, PIECES)),
            dma((2, 2, 2, 2)),
            dma((3, 2, 2)),
            dma((4,)),
            dma((4, 3)),
            dma((4, 3)),
            dma((2,)),
            dma((2, 4)),
            dma((2,)),
            dma((4, 2, 2)),
            dma((2, 2, 2)),
            dma((2,)),
        ],
        compiler_params=pltpu.CompilerParams(
            collective_id=0, has_side_effects=True, vmem_limit_bytes=60 * 2**20
        ),
    )(
        embedded,
        w_qkv.reshape(WIDTH, 512),
        w_out,
        gates,
        norm_gain.astype(F32).reshape(4, 1024),
        head_gain,
        gate_bias,
        owner,
    )
    memory_c = mem[None, None, None]
    memory_n = aux[0][None, None, None]
    memory_m = aux[1, 0:1][None, None]
    return (block_out, memory_c, memory_n, memory_m)


def solution(mesh):
    return jax.shard_map(
        local,
        mesh=mesh,
        in_specs=(
            P(None, "ctx"),
            P(None, "hr"),
            P(),
            P(None, "hr", None, None),
            P(),
            P(),
            P(),
            P(None, "hr"),
            P(),
        ),
        out_specs=(
            P(None, "ctx", "hr"),
            P("ctx", "hr", None, None, None),
            P("ctx", "hr", None, None),
            P("ctx", "hr", None),
        ),
        check_vma=False,
    )
```

time: 234 us -> 187 us (0.80); the launches traced: 230 us -> 187 us
  Pallas kernels: 192 us -> 161 us
  other arithmetic: 12.3 us -> 0.71 us
  between operations: 3.12 us -> 0.64 us
    pallas_call x1, Pallas kernels: 192 us -> 161 us  [local(): pl.pallas_call(kernel, out_shape=(jax.ShapeDtypeStruct((2, ROWS, 256), BF...]
    convert_element_type x6 -> x0, other arithmetic: 8.49 us -> none  [the longest x1 2.46 us: local(): block_out = (embedded.astype(F32) + rows.astype(F32)).astype(BF16)]
    unnamed x4 -> x2, local copies, waits for them, and re-layouts: 0.67 us -> 4.13 us
where the time goes in v2:
time: 187 us
  Pallas kernels  161 us (86%)
  local copies, waits for them, and re-layouts  24.3 us (13%)
    pallas_call x1, Pallas kernels, local(): pl.pallas_call(kernel, out_shape=(jax.ShapeDtypeStruct((2, ROWS, 256), BF...  161 us
    gather x1, local copies, waits for them, and re-layouts, local(): embedded = embed_table.at[token_ids].get(mode='promise_in_bounds')  16.4 us
    unnamed x2, local copies, waits for them, and re-layouts  4.13 us

profile of v2, /device:TPU:8, one launch (start us, length us, event | category | flops | bytes accessed | tf_op | source)
XLA Modules:
  0.0 187.0 jit_solution(5142666007106723333)
XLA Ops:
  0.6 0.7 fusion
  1.3 1.3 reshape.24.norm_gain
  2.7 16.4 %gather_fusion = bf16[2048,256]{1,0:T(8,128)(2,1)} fusion(bf16[32768,256]{1,0:T(8,128)(2,1)} %param.10, s32[2048]{0:T(1024)S(1)} %bitcast_clamp_fusion), kind=kCustom, calls=%fused_computation | custom fusion | bytes 2105344 | tf_op jit(solution)/shard_map/gather | solution.py:573
  19.1 161.3 %shard_map.120 = (bf16[2,1024,256]{2,1,0:T(8,128)(2,1)}, f32[256,512]{1,0:T(8,128)}, f32[8,256]{1,0:T(8,128)}) custom-call(bf16[2,1024,256]{2,1,0:T(8,128)(2,1)} %bitcast.14, bf16[4096,512]{1,0:T(8,128)(2,1)} %bitcast.13, bf16[4096,256]{1,0:T(8,128)(2,1)} %w_out.1, bf16[16,4096]{1,0:T(8,128)(2,1)} %bitcast.16, f32[4,1024]{1,0:T(4,128)} %reshape.24.norm_gain, ...), custom_call_target="tpu_custom_call" | custom-call | tf_op jit(solution)/shard_map/pallas_call | solution.py:579
  180.4 1.2 slice.7
  181.6 1.3 slice_bitcast_fusion
  182.9 2.3 %copy.17 = bf16[2,1024,256]{2,1,0:T(8,128)(2,1)} copy(bf16[2,1024,256]{2,1,0:T(8,128)(2,1)} %get-tuple-element.14) | data formatting | bytes 2097152
  185.2 1.9 copy.18
  (1 shorter events, 0.0 us)

commit v3 on v2

--- a/solution.py
+++ b/solution.py
@@ -19,8 +19,8 @@
 KEY = 256
 VAL = 512
 SENDS = 128
-SPREAD = 320
-DIRECT = 768
+SPREAD = 384
+DIRECT = 512
 TILE = 256
 
 
@@ -33,7 +33,8 @@
 
 
 def kernel(
-    emb,
+    ids,
+    table,
     w_own,
     w_out,
     w_gate,
@@ -44,6 +45,8 @@
     out,
     out_mem,
     out_aux,
+    tbl,
+    emb,
     xb,
     wb,
     wo,
@@ -51,6 +54,7 @@
     ks,
     vs,
     gs,
+    scales,
     num,
     den,
     rows_in,
@@ -70,6 +74,7 @@
     aux_out,
     send_sem,
     local_sem,
+    sem_tbl,
     sem_a,
     sem_ring,
     sem_sib,
@@ -103,6 +108,12 @@
     z_next, z_prev = dev(x, y, rel(z, 1), k), dev(x, y, rel(z, 3), k)
     mate = dev(x, 2 * req + 1 - par, z, k)
 
+    copies = []
+    for part in range(4):
+        rows = pl.ds(part * 1024, 1024)
+        copies.append(pltpu.make_async_copy(table.at[rows], tbl.at[rows], sem_tbl.at[part]))
+        copies[-1].start()
+
     partners = [sib]
     for step in (1, 2, 3):
         for core in (0, 1):
@@ -154,21 +165,42 @@
     xl, xr, xo = rel(x, 3), rel(x, 1), rel(x, 2)
     zl, zr, zo = rel(z, 3), rel(z, 1), rel(z, 2)
 
-    for piece in range(PIECES):
+    sub_tile = lax.broadcasted_iota(jnp.int32, (8, 256), 0)
+
+    def look(r_, start):
+        def body(step, carry):
+            base = pl.multiple_of(start + step * 16, 16)
+            eights = []
+            for eight in (0, 1):
+                found = jnp.zeros((8, 256), F32)
+                for t in range(8):
+                    token = ids[r_, base + eight * 8 + t]
+                    turned = pltpu.roll(
+                        tbl[lax.shift_right_logical(token, 3)].astype(F32),
+                        lax.rem(t + 8 - lax.rem(token, 8), 8),
+                        0,
+                    )
+                    found = jnp.where(sub_tile == t, turned, found)
+                eights.append(found)
+            emb[r_, pl.ds(base, 16), :] = jnp.concatenate(eights, axis=0).astype(BF16)
+            return carry
+
+        lax.fori_loop(0, PIECE // 16, body, 0)
+
+    def look_and_send(piece):
         for r_ in (0, 1):
             for kd in (0, 1):
                 y_to = 2 * r_ + k
                 mine = (y_to == y) & (kd == k)
                 start = kd * HALF + piece * PIECE
+                look(r_, start)
                 src = emb.at[r_, pl.ds(start, PIECE), :]
                 dst = xb.at[x, pl.ds(start, PIECE), pl.ds(pl.multiple_of(y * 256, 256), 256)]
                 push(src, dst, sem_a.at[piece, y], dev(x, y_to, z, kd), jnp.logical_not(mine))
                 here(src, dst, sem_a.at[piece, y], mine)
 
     w_local = pltpu.make_async_copy(w_own, wb.at[y % 2], local_sem.at[0])
-    pl.when(k == y // 2)(w_local.start)
     o_local = pltpu.make_async_copy(w_out, wo.at[y], local_sem.at[1])
-    o_local.start()
 
     def rows_of(block, core, piece, half=None):
         start, size = core * HALF + piece * PIECE, PIECE
@@ -256,15 +288,21 @@
                 push(block, block, sem_wz.at[0, j, part], z_next, right)
                 push(block, block, sem_wz.at[1, j, part], z_prev, right)
 
-    ring_start(0)
     w_send(0)
-    ring_start(1)
+    for copy in copies:
+        copy.wait()
+    pl.when(k == y // 2)(w_local.start)
+    o_local.start()
+    look_and_send(0)
     w_near(0)
     w_along_z((1, 3))
-    w_send(1)
-    ring_middle(0)
+    look_and_send(1)
+    ring_start(0)
     w_far(0)
     w_along_z((2,))
+    w_send(1)
+    ring_start(1)
+    ring_middle(0)
     ring_middle(1)
     w_near(1)
 
@@ -312,6 +350,10 @@
         for piece in range(PIECES):
             arrived(rows_of(block_x, 1 - k, piece), sem_sib.at[index, piece])
 
+    def norm(block, rows, scale):
+        wide = xb[block, rows, :].astype(F32)
+        return (wide * scale * norm_gain[block : block + 1, :]).astype(BF16)
+
     def project(step, carry):
         rows = pl.ds(pl.multiple_of(step * TILE, TILE), TILE)
         squares = jnp.zeros((TILE, 1), F32)
@@ -319,19 +361,28 @@
             wide = xb[block, rows, :].astype(F32)
             squares += jnp.sum(wide * wide, axis=1, keepdims=True)
         scale = lax.rsqrt(squares / WIDTH + epsilon)
-        accs = [jnp.zeros((TILE, 512), F32), jnp.zeros((TILE, 512), F32)]
+        scales[rows, :] = jnp.broadcast_to(scale, (TILE, 128))
+        keys, values = jnp.zeros((TILE, KEY), F32), jnp.zeros((TILE, VAL), F32)
         gate = jnp.zeros((16, TILE), F32)
         for block in range(4):
             depth = slice(block * 1024, block * 1024 + 1024)
-            wide = xb[block, rows, :].astype(F32)
-            normed = (wide * scale * norm_gain[block : block + 1, :]).astype(BF16)
-            for j in (0, 1):
-                accs[j] = accs[j] + dot(normed, wb[j, depth, :])
+            normed = norm(block, rows, scale)
+            keys = keys + dot(normed, wb[0, depth, KEY:])
+            values = values + dot(normed, wb[1, depth, :])
             gate = gate + dot_t(w_gate[:, depth], normed)
-        qs[rows, :] = accs[0][:, :KEY].astype(BF16)
-        ks[rows, :] = accs[0][:, KEY:].astype(BF16)
-        vs[rows, :] = accs[1].astype(BF16)
+        ks[rows, :] = keys.astype(BF16)
+        vs[rows, :] = values.astype(BF16)
         gs[:, rows] = gate
+        return carry
+
+    def project_queries(step, carry):
+        rows = pl.ds(pl.multiple_of(step * TILE, TILE), TILE)
+        scale = scales[rows, :][:, 0:1]
+        queries = jnp.zeros((TILE, KEY), F32)
+        for block in range(4):
+            normed = norm(block, rows, scale)
+            queries = queries + dot(normed, wb[0, block * 1024 : block * 1024 + 1024, :KEY])
+        qs[rows, :] = queries.astype(BF16)
         return carry
 
     lax.fori_loop(0, ROWS // TILE, project, 0)
@@ -376,6 +427,8 @@
     push(sum_aux.at[par], sum_aux.at[par], sem_mate.at[0], mate)
     push(sum_c.at[par], sum_c.at[par], sem_mate.at[1], mate)
 
+    lax.fori_loop(0, ROWS // TILE, project_queries, 0)
+
     lead_row = rows_in[8:9, :]
 
     def within(index):
@@ -406,8 +459,6 @@
         zero = jnp.zeros((1, KEY), F32)
         return zero, jnp.full((1, KEY), very_negative, F32), zero
 
-    for index in (0, 1):
-        within(index)
     other = 1 - par
     arrived(sum_aux.at[other], sem_mate.at[0])
     arrived(sum_c.at[other], sem_mate.at[1])
@@ -420,7 +471,7 @@
         to = dev(x, y, rel(z, step), k)
         push(pair_aux.at[z], pair_aux.at[z], sem_pair.at[0, z], to)
         push(pair_c.at[z], pair_c.at[z], sem_pair.at[1, z], to)
-    for index in (2, 3):
+    for index in range(4):
         within(index)
 
     for step in (1, 3, 2):
@@ -569,8 +620,14 @@
             pl.when(when)(copy.wait_send)
 
 
+def tail(rows, mem, aux, out, out_c, out_n, out_m):
+    out[...] = rows[...]
+    out_c[...] = mem[...]
+    out_n[...] = aux[0:1, :]
+    out_m[...] = aux[1:2, 0:1]
+
+
 def local(token_ids, embed_table, norm_gain, w_qkv, w_gate, gate_bias, head_gain, w_out, owner):
-    embedded = embed_table.at[token_ids].get(mode="promise_in_bounds")
     gates = jnp.transpose(w_gate, (1, 2, 0)).reshape(16, WIDTH)
     vmem = pl.BlockSpec(memory_space=pltpu.VMEM)
     smem = pl.BlockSpec(memory_space=pltpu.SMEM)
@@ -583,9 +640,11 @@
             jax.ShapeDtypeStruct((KEY, VAL), F32),
             jax.ShapeDtypeStruct((8, KEY), F32),
         ),
-        in_specs=[vmem, hbm, hbm, vmem, vmem, vmem, smem, smem],
+        in_specs=[smem, hbm, hbm, hbm, vmem, vmem, vmem, smem, smem],
         out_specs=(vmem, vmem, vmem),
         scratch_shapes=[
+            pltpu.VMEM((4096, 8, 256), BF16),
+            pltpu.VMEM((2, ROWS, 256), BF16),
             pltpu.VMEM((4, ROWS, 1024), BF16),
             pltpu.VMEM((2, WIDTH, 512), BF16),
             pltpu.VMEM((4, WIDTH, 256), BF16),
@@ -593,6 +652,7 @@
             pltpu.VMEM((ROWS, KEY), BF16),
             pltpu.VMEM((ROWS, VAL), BF16),
             pltpu.VMEM((16, ROWS), F32),
+            pltpu.VMEM((ROWS, 128), F32),
             pltpu.VMEM((ROWS, VAL), F32),
             pltpu.VMEM((ROWS, 128), F32),
             pltpu.VMEM((128, ROWS), F32),
@@ -612,6 +672,7 @@
             pltpu.VMEM((8, KEY), F32),
             dma((SENDS,)),
             dma((2,)),
+            dma((4,)),
             dma((PIECES, 4)),
             dma((4, PIECES)),
             dma((4, PIECES)),
@@ -628,10 +689,11 @@
             dma((2,)),
         ],
         compiler_params=pltpu.CompilerParams(
-            collective_id=0, has_side_effects=True, vmem_limit_bytes=60 * 2**20
+            collective_id=0, has_side_effects=True, vmem_limit_bytes=62 * 2**20
         ),
     )(
-        embedded,
+        token_ids,
+        embed_table.reshape(4096, 8, 256),
         w_qkv.reshape(WIDTH, 512),
         w_out,
         gates,
@@ -640,9 +702,20 @@
         gate_bias,
         owner,
     )
-    memory_c = mem[None, None, None]
-    memory_n = aux[0][None, None, None]
-    memory_m = aux[1, 0:1][None, None]
+    block_out, memory_c, memory_n, memory_m = pl.pallas_call(
+        tail,
+        out_shape=(
+            jax.ShapeDtypeStruct((2, ROWS, 256), BF16),
+            jax.ShapeDtypeStruct((KEY, VAL), F32),
+            jax.ShapeDtypeStruct((1, KEY), F32),
+            jax.ShapeDtypeStruct((1, 1), F32),
+        ),
+        in_specs=[vmem, vmem, vmem],
+        out_specs=(vmem, vmem, vmem, vmem),
+    )(block_out, mem, aux)
+    memory_c = memory_c[None, None, None]
+    memory_n = memory_n[None, None]
+    memory_m = memory_m[None]
     return (block_out, memory_c, memory_n, memory_m)
 
 

time: 187 us -> 160 us (0.86)
  local copies, waits for them, and re-layouts: 24.3 us -> 1.31 us
  Pallas kernels: 161 us -> 157 us
    gather x1 -> x0, local copies, waits for them, and re-layouts: 16.4 us -> none  [local(): embedded = embed_table.at[token_ids].get(mode='promise_in_bounds')]
    pallas_call x1, Pallas kernels: 161 us -> 155 us  [local(): pl.pallas_call(kernel, out_shape=(jax.ShapeDtypeStruct((2, ROWS, 256), BF...]
    unnamed x2 -> x0, local copies, waits for them, and re-layouts: 4.13 us -> none
    pallas_call x0 -> x1, Pallas kernels: none -> 2.57 us  [local(): pl.pallas_call(tail, out_shape=(jax.ShapeDtypeStruct((2, ROWS, 256), BF16...]
where the time goes in v3:
time: 160 us; the launch traced here: 159 us
  Pallas kernels  157 us (98%)
    pallas_call x1, Pallas kernels, local(): pl.pallas_call(kernel, out_shape=(jax.ShapeDtypeStruct((2, ROWS, 256), BF...  155 us

profile of v3, /device:TPU:8, one launch (start us, length us, event | category | flops | bytes accessed | tf_op | source)
XLA Modules:
  0.0 159.4 jit_solution(10551704789175856719)
XLA Ops:
  0.6 1.3 reshape.28.norm_gain
  1.9 154.8 %shard_map.120 = (bf16[2,1024,256]{2,1,0:T(8,128)(2,1)}, f32[256,512]{1,0:T(8,128)}, f32[8,256]{1,0:T(8,128)}) custom-call(s32[2,1024]{1,0:T(2,128)} %ids.1, bf16[4096,8,256]{2,1,0:T(8,128)(2,1)} %bitcast.8, bf16[4096,512]{1,0:T(8,128)(2,1)} %bitcast.9, bf16[4096,256]{1,0:T(8,128)(2,1)} %w_out.1, bf16[16,4096]{1,0:T(8,128)(2,1)} %bitcast.10, ...), custom_call_target="tpu_custom_call" | custom-call | tf_op jit(solution)/shard_map/pallas_call | solution.py:636
  156.8 2.6 %shard_map.121 = (bf16[2,1024,256]{2,1,0:T(8,128)(2,1)}, f32[256,512]{1,0:T(8,128)}, f32[1,256]{1,0:T(1,128)}, f32[1,1]{1,0:T(1,128)}) custom-call(bf16[2,1024,256]{2,1,0:T(8,128)(2,1)} %get-tuple-element.11.rows, f32[256,512]{1,0:T(8,128)} %get-tuple-element.12.mem, f32[8,256]{1,0:T(8,128)} %get-tuple-element.13.aux), custom_call_target="tpu_custom_call" | custom-call | tf_op jit(solution)/shard_map/pallas_call | solution.py:705

commit v4 on v3

--- a/solution.py
+++ b/solution.py
@@ -14,11 +14,11 @@
 WIDTH = 4096
 ROWS = 1024
 HALF = 512
-PIECES = 2
+PIECES = 4
 PIECE = HALF // PIECES
 KEY = 256
 VAL = 512
-SENDS = 128
+SENDS = 192
 SPREAD = 384
 DIRECT = 512
 TILE = 256
@@ -195,7 +195,7 @@
                 start = kd * HALF + piece * PIECE
                 look(r_, start)
                 src = emb.at[r_, pl.ds(start, PIECE), :]
-                dst = xb.at[x, pl.ds(start, PIECE), pl.ds(pl.multiple_of(y * 256, 256), 256)]
+                dst = xb.at[x, piece, kd, :, pl.ds(pl.multiple_of(y * 256, 256), 256)]
                 push(src, dst, sem_a.at[piece, y], dev(x, y_to, z, kd), jnp.logical_not(mine))
                 here(src, dst, sem_a.at[piece, y], mine)
 
@@ -203,15 +203,14 @@
     o_local = pltpu.make_async_copy(w_out, wo.at[y], local_sem.at[1])
 
     def rows_of(block, core, piece, half=None):
-        start, size = core * HALF + piece * PIECE, PIECE
-        if half is not None:
-            start, size = start + half * (PIECE // 2), PIECE // 2
-        return xb.at[block, pl.ds(start, size), :]
+        if half is None:
+            return xb.at[block, piece, core]
+        return xb.at[block, piece, core, pl.ds(half * (PIECE // 2), PIECE // 2), :]
 
     def ring_start(piece):
         for y_ in range(4):
             arrived(
-                xb.at[x, pl.ds(k_half + piece * PIECE, PIECE), pl.ds(y_ * 256, 256)],
+                xb.at[x, piece, k, :, pl.ds(y_ * 256, 256)],
                 sem_a.at[piece, y_],
             )
         block = rows_of(x, k, piece)
@@ -237,7 +236,7 @@
         block = rows_of(xo, k, piece)
         push(block, block, sem_sib.at[3, piece], sib)
 
-    def w_part(kind, j, plane, part, half=None):
+    def w_part(late, kind, j, plane, part, half=None):
         if kind == 0:
             start, size = (plane * 2 + part) * SPREAD, SPREAD
         else:
@@ -245,147 +244,181 @@
         if half is not None:
             start, size = start + half * (size // 2), size // 2
         if not isinstance(start, int):
-            start = pl.multiple_of(start, 32)
-        return (j, pl.ds(start, size), slice(None))
-
-    def w_send(kind):
-        at = w_part(kind, y % 2, z, k)
-        src = w_own.at[at[1], at[2]]
+            start = pl.multiple_of(start, 64)
+        cols = slice(None)
+        if j == 0:
+            cols = pl.ds(0 if late else KEY, KEY)
+        return (j, pl.ds(start, size), cols)
+
+    def w_send(late, kind):
         core = y // 2
-        push(src, wb.at[at], sem_w.at[kind, y % 2, k, 0], dev(x, rel(y, 1), z, core))
-        push(src, wb.at[at], sem_w.at[kind, y % 2, k, 0], dev(x, rel(y, 3), z, core))
+        for j in (0,) if late else (0, 1):
+            at = w_part(late, kind, j, z, k)
+            src = w_own.at[at[1], at[2]]
+            mine = y % 2 == j
+            push(src, wb.at[at], sem_w.at[late, kind, j, k, 0], dev(x, rel(y, 1), z, core), mine)
+            push(src, wb.at[at], sem_w.at[late, kind, j, k, 0], dev(x, rel(y, 3), z, core), mine)
 
     away = [lax.rem(y - 2 * k - j + 4, 4) for j in (0, 1)]
     foreign = [step != 0 for step in away]
 
-    def w_near(kind):
-        for j in (0, 1):
+    def w_near(late, kind):
+        for j in (0,) if late else (0, 1):
             near = (away[j] == 1) | (away[j] == 3)
             for part in (0, 1):
-                arrived(wb.at[w_part(kind, j, z, part)], sem_w.at[kind, j, part, 0], near)
-                half = wb.at[w_part(kind, j, z, part, 0)]
-                push(half, half, sem_w.at[kind, j, part, 0], y_next, away[j] == 1)
-                half = wb.at[w_part(kind, j, z, part, 1)]
-                push(half, half, sem_w.at[kind, j, part, 1], y_prev, away[j] == 3)
-
-    def w_far(kind):
-        for j in (0, 1):
+                sems = sem_w.at[late, kind, j, part]
+                arrived(wb.at[w_part(late, kind, j, z, part)], sems.at[0], near)
+                half = wb.at[w_part(late, kind, j, z, part, 0)]
+                push(half, half, sems.at[0], y_next, away[j] == 1)
+                half = wb.at[w_part(late, kind, j, z, part, 1)]
+                push(half, half, sems.at[1], y_prev, away[j] == 3)
+                if kind == 0:
+                    w_along_z(late, j, part, near)
+
+    def w_far(late, kind):
+        for j in (0,) if late else (0, 1):
+            far = away[j] == 2
             for part in (0, 1):
                 for half in (0, 1):
                     arrived(
-                        wb.at[w_part(kind, j, z, part, half)],
-                        sem_w.at[kind, j, part, half],
-                        away[j] == 2,
+                        wb.at[w_part(late, kind, j, z, part, half)],
+                        sem_w.at[late, kind, j, part, half],
+                        far,
                     )
-
-    def w_along_z(distances):
-        for j in (0, 1):
-            right = away[j] == distances[0]
-            for other in distances[1:]:
-                right = right | (away[j] == other)
+                if kind == 0:
+                    w_along_z(late, j, part, far)
+
+    def w_along_z(late, j, part, when):
+        block = wb.at[w_part(late, 0, j, z, part)]
+        push(block, block, sem_wz.at[late, 0, j, part], z_next, when)
+        push(block, block, sem_wz.at[late, 1, j, part], z_prev, when)
+
+    def w_middle(late):
+        for j in (0,) if late else (0, 1):
             for part in (0, 1):
-                block = wb.at[w_part(0, j, z, part)]
-                push(block, block, sem_wz.at[0, j, part], z_next, right)
-                push(block, block, sem_wz.at[1, j, part], z_prev, right)
-
-    w_send(0)
+                from_left = wb.at[w_part(late, 0, j, zl, part)]
+                from_right = wb.at[w_part(late, 0, j, zr, part)]
+                arrived(from_left, sem_wz.at[late, 0, j, part], foreign[j])
+                arrived(from_right, sem_wz.at[late, 1, j, part], foreign[j])
+                if part == 0:
+                    push(from_left, from_left, sem_wz.at[late, 2, j, 0], z_next, foreign[j])
+                else:
+                    push(from_right, from_right, sem_wz.at[late, 2, j, 1], z_prev, foreign[j])
+
+    def w_end(late):
+        for j in (0,) if late else (0, 1):
+            for part in (0, 1):
+                arrived(
+                    wb.at[w_part(late, 0, j, zo, part)], sem_wz.at[late, 2, j, part], foreign[j]
+                )
+
+    def o_part(y_, plane, core, half=None):
+        start, size = plane * 1024 + core * 512, 512
+        if half is not None:
+            start, size = start + half * 256, 256
+        return wo.at[y_, pl.ds(pl.multiple_of(start, 256), size), :]
+
+    def o_send():
+        for step in (1, 3, 2):
+            push(
+                w_out.at[pl.ds(pl.multiple_of(z * 1024 + k * 512, 512), 512), :],
+                o_part(y, z, k),
+                sem_wo.at[y],
+                dev(x, rel(y, step), z, k),
+            )
+
+    others = [rel(y, step) for step in (1, 2, 3)]
+
+    def o_along_z():
+        for index, y_ in enumerate(others):
+            block = o_part(y_, z, k)
+            arrived(block, sem_wo.at[y_])
+            push(block, block, sem_woz.at[0, index], z_next)
+            push(block, block, sem_woz.at[1, index], z_prev)
+            push(block, block, sem_wos.at[0, index], sib)
+
+    def norm(block, piece, scale):
+        wide = xb[block, piece].astype(F32).reshape(2 * PIECE, 1024)
+        return (wide * scale * norm_gain[block : block + 1, :]).astype(BF16)
+
+    def spread(target, piece, value):
+        for core in (0, 1):
+            start = core * HALF + piece * PIECE
+            target[start : start + PIECE, :] = value[core * PIECE : (core + 1) * PIECE, :]
+
+    def project(piece):
+        for index, block_x in enumerate((x, xl, xr, xo)):
+            arrived(rows_of(block_x, 1 - k, piece), sem_sib.at[index, piece])
+        squares = jnp.zeros((2 * PIECE, 1), F32)
+        for block in range(4):
+            wide = xb[block, piece].astype(F32).reshape(2 * PIECE, 1024)
+            squares += jnp.sum(wide * wide, axis=1, keepdims=True)
+        scale = lax.rsqrt(squares / WIDTH + epsilon)
+        scales[piece] = jnp.broadcast_to(scale, (2 * PIECE, 128))
+        keys, values = jnp.zeros((2 * PIECE, KEY), F32), jnp.zeros((2 * PIECE, VAL), F32)
+        gate = jnp.zeros((16, 2 * PIECE), F32)
+        for block in range(4):
+            depth = slice(block * 1024, block * 1024 + 1024)
+            normed = norm(block, piece, scale)
+            keys = keys + dot(normed, wb[0, depth, KEY:])
+            values = values + dot(normed, wb[1, depth, :])
+            gate = gate + dot_t(w_gate[:, depth], normed)
+        spread(ks, piece, keys.astype(BF16))
+        spread(vs, piece, values.astype(BF16))
+        for core in (0, 1):
+            start = core * HALF + piece * PIECE
+            gs[:, start : start + PIECE] = gate[:, core * PIECE : (core + 1) * PIECE]
+
+    def project_queries(piece):
+        scale = scales[piece][:, 0:1]
+        queries = jnp.zeros((2 * PIECE, KEY), F32)
+        for block in range(4):
+            normed = norm(block, piece, scale)
+            queries = queries + dot(normed, wb[0, block * 1024 : block * 1024 + 1024, :KEY])
+        spread(qs, piece, queries.astype(BF16))
+
+    w_send(0, 0)
     for copy in copies:
         copy.wait()
     pl.when(k == y // 2)(w_local.start)
     o_local.start()
     look_and_send(0)
-    w_near(0)
-    w_along_z((1, 3))
     look_and_send(1)
+    w_near(0, 0)
+    look_and_send(2)
     ring_start(0)
-    w_far(0)
-    w_along_z((2,))
-    w_send(1)
+    look_and_send(3)
+    w_far(0, 0)
+    w_send(0, 1)
     ring_start(1)
+    ring_start(2)
     ring_middle(0)
+    ring_start(3)
     ring_middle(1)
-    w_near(1)
-
-    def o_part(y_, plane, core, half=None):
-        start, size = plane * 1024 + core * 512, 512
-        if half is not None:
-            start, size = start + half * 256, 256
-        return wo.at[y_, pl.ds(pl.multiple_of(start, 256), size), :]
-
-    for step in (1, 3, 2):
-        push(
-            w_out.at[pl.ds(pl.multiple_of(z * 1024 + k * 512, 512), 512), :],
-            o_part(y, z, k),
-            sem_wo.at[y],
-            dev(x, rel(y, step), z, k),
-        )
-
-    for j in (0, 1):
-        for part in (0, 1):
-            from_left, from_right = wb.at[w_part(0, j, zl, part)], wb.at[w_part(0, j, zr, part)]
-            arrived(from_left, sem_wz.at[0, j, part], foreign[j])
-            arrived(from_right, sem_wz.at[1, j, part], foreign[j])
-            if part == 0:
-                push(from_left, from_left, sem_wz.at[2, j, 0], z_next, foreign[j])
-            else:
-                push(from_right, from_right, sem_wz.at[2, j, 1], z_prev, foreign[j])
-
+    w_near(0, 1)
+    w_send(1, 0)
+    w_send(1, 1)
+    w_middle(0)
+    ring_middle(2)
     ring_end(0)
+    ring_middle(3)
     ring_end(1)
-    w_far(1)
+    w_far(0, 1)
+    o_send()
+    w_near(1, 0)
+    w_near(1, 1)
     pl.when(k == y // 2)(w_local.wait)
-    for j in (0, 1):
-        for part in (0, 1):
-            arrived(wb.at[w_part(0, j, zo, part)], sem_wz.at[2, j, part], foreign[j])
-
-    others = [rel(y, step) for step in (1, 2, 3)]
-    for index, y_ in enumerate(others):
-        block = o_part(y_, z, k)
-        arrived(block, sem_wo.at[y_])
-        push(block, block, sem_woz.at[0, index], z_next)
-        push(block, block, sem_woz.at[1, index], z_prev)
-        push(block, block, sem_wos.at[0, index], sib)
-
-    for index, block_x in enumerate((x, xl, xr, xo)):
-        for piece in range(PIECES):
-            arrived(rows_of(block_x, 1 - k, piece), sem_sib.at[index, piece])
-
-    def norm(block, rows, scale):
-        wide = xb[block, rows, :].astype(F32)
-        return (wide * scale * norm_gain[block : block + 1, :]).astype(BF16)
-
-    def project(step, carry):
-        rows = pl.ds(pl.multiple_of(step * TILE, TILE), TILE)
-        squares = jnp.zeros((TILE, 1), F32)
-        for block in range(4):
-            wide = xb[block, rows, :].astype(F32)
-            squares += jnp.sum(wide * wide, axis=1, keepdims=True)
-        scale = lax.rsqrt(squares / WIDTH + epsilon)
-        scales[rows, :] = jnp.broadcast_to(scale, (TILE, 128))
-        keys, values = jnp.zeros((TILE, KEY), F32), jnp.zeros((TILE, VAL), F32)
-        gate = jnp.zeros((16, TILE), F32)
-        for block in range(4):
-            depth = slice(block * 1024, block * 1024 + 1024)
-            normed = norm(block, rows, scale)
-            keys = keys + dot(normed, wb[0, depth, KEY:])
-            values = values + dot(normed, wb[1, depth, :])
-            gate = gate + dot_t(w_gate[:, depth], normed)
-        ks[rows, :] = keys.astype(BF16)
-        vs[rows, :] = values.astype(BF16)
-        gs[:, rows] = gate
-        return carry
-
-    def project_queries(step, carry):
-        rows = pl.ds(pl.multiple_of(step * TILE, TILE), TILE)
-        scale = scales[rows, :][:, 0:1]
-        queries = jnp.zeros((TILE, KEY), F32)
-        for block in range(4):
-            normed = norm(block, rows, scale)
-            queries = queries + dot(normed, wb[0, block * 1024 : block * 1024 + 1024, :KEY])
-        qs[rows, :] = queries.astype(BF16)
-        return carry
-
-    lax.fori_loop(0, ROWS // TILE, project, 0)
+    w_end(0)
+    project(0)
+    ring_end(2)
+    project(1)
+    w_far(1, 0)
+    ring_end(3)
+    project(2)
+    project(3)
+    w_middle(1)
+    w_far(1, 1)
+    o_along_z()
 
     head = 2 * x + k
     gates = gs[...]
@@ -427,7 +460,9 @@
     push(sum_aux.at[par], sum_aux.at[par], sem_mate.at[0], mate)
     push(sum_c.at[par], sum_c.at[par], sem_mate.at[1], mate)
 
-    lax.fori_loop(0, ROWS // TILE, project_queries, 0)
+    w_end(1)
+    for piece in range(PIECES):
+        project_queries(piece)
 
     lead_row = rows_in[8:9, :]
 
@@ -645,14 +680,14 @@
         scratch_shapes=[
             pltpu.VMEM((4096, 8, 256), BF16),
             pltpu.VMEM((2, ROWS, 256), BF16),
-            pltpu.VMEM((4, ROWS, 1024), BF16),
+            pltpu.VMEM((4, PIECES, 2, PIECE, 1024), BF16),
             pltpu.VMEM((2, WIDTH, 512), BF16),
             pltpu.VMEM((4, WIDTH, 256), BF16),
             pltpu.VMEM((ROWS, KEY), BF16),
             pltpu.VMEM((ROWS, KEY), BF16),
             pltpu.VMEM((ROWS, VAL), BF16),
             pltpu.VMEM((16, ROWS), F32),
-            pltpu.VMEM((ROWS, 128), F32),
+            pltpu.VMEM((PIECES, 2 * PIECE, 128), F32),
             pltpu.VMEM((ROWS, VAL), F32),
             pltpu.VMEM((ROWS, 128), F32),
             pltpu.VMEM((128, ROWS), F32),
@@ -676,8 +711,8 @@
             dma((PIECES, 4)),
             dma((4, PIECES)),
             dma((4, PIECES)),
-            dma((2, 2, 2, 2)),
-            dma((3, 2, 2)),
+            dma((2, 2, 2, 2, 2)),
+            dma((2, 3, 2, 2)),
             dma((4,)),
             dma((4, 3)),
             dma((4, 3)),

time: 160 us -> 170 us (1.062)
  Pallas kernels: 157 us -> 166 us
    pallas_call x1, Pallas kernels: 155 us -> 163 us  [local(): pl.pallas_call(kernel, out_shape=(jax.ShapeDtypeStruct((2, ROWS, 256), BF...]
where the time goes in v4:
time: 170 us; the launch traced here: 168 us
  Pallas kernels  166 us (98%)
    pallas_call x1, Pallas kernels, local(): pl.pallas_call(kernel, out_shape=(jax.ShapeDtypeStruct((2, ROWS, 256), BF...  163 us

profile of v4, /device:TPU:8, one launch (start us, length us, event | category | flops | bytes accessed | tf_op | source)
XLA Modules:
  0.0 167.9 jit_solution(2751119701115926322)
XLA Ops:
  0.6 1.3 reshape.28.norm_gain
  1.9 163.4 %shard_map.120 = (bf16[2,1024,256]{2,1,0:T(8,128)(2,1)}, f32[256,512]{1,0:T(8,128)}, f32[8,256]{1,0:T(8,128)}) custom-call(s32[2,1024]{1,0:T(2,128)} %ids.1, bf16[4096,8,256]{2,1,0:T(8,128)(2,1)} %bitcast.8, bf16[4096,512]{1,0:T(8,128)(2,1)} %bitcast.9, bf16[4096,256]{1,0:T(8,128)(2,1)} %w_out.1, bf16[16,4096]{1,0:T(8,128)(2,1)} %bitcast.10, ...), custom_call_target="tpu_custom_call" | custom-call | tf_op jit(solution)/shard_map/pallas_call | solution.py:671
  165.3 2.6 %shard_map.121 = (bf16[2,1024,256]{2,1,0:T(8,128)(2,1)}, f32[256,512]{1,0:T(8,128)}, f32[1,256]{1,0:T(1,128)}, f32[1,1]{1,0:T(1,128)}) custom-call(bf16[2,1024,256]{2,1,0:T(8,128)(2,1)} %get-tuple-element.11.rows, f32[256,512]{1,0:T(8,128)} %get-tuple-element.12.mem, f32[8,256]{1,0:T(8,128)} %get-tuple-element.13.aux), custom_call_target="tpu_custom_call" | custom-call | tf_op jit(solution)/shard_map/pallas_call | solution.py:740

commit v5 on v4

--- a/solution.py
+++ b/solution.py
@@ -19,8 +19,10 @@
 KEY = 256
 VAL = 512
 SENDS = 192
-SPREAD = 384
-DIRECT = 512
+SPREAD = 320
+DIRECT = 768
+O_SPREAD = 256
+O_DIRECT = 1024
 TILE = 256
 
 
@@ -69,6 +71,7 @@
     own_p,
     total,
     rows_got,
+    mem_out,
     mem_got,
     aux_got,
     aux_out,
@@ -236,7 +239,7 @@
         block = rows_of(xo, k, piece)
         push(block, block, sem_sib.at[3, piece], sib)
 
-    def w_part(late, kind, j, plane, part, half=None):
+    def w_part(kind, j, plane, part, half=None):
         if kind == 0:
             start, size = (plane * 2 + part) * SPREAD, SPREAD
         else:
@@ -244,98 +247,120 @@
         if half is not None:
             start, size = start + half * (size // 2), size // 2
         if not isinstance(start, int):
-            start = pl.multiple_of(start, 64)
-        cols = slice(None)
-        if j == 0:
-            cols = pl.ds(0 if late else KEY, KEY)
-        return (j, pl.ds(start, size), cols)
-
-    def w_send(late, kind):
+            start = pl.multiple_of(start, 32)
+        return (j, pl.ds(start, size), slice(None))
+
+    def w_send(kind):
         core = y // 2
-        for j in (0,) if late else (0, 1):
-            at = w_part(late, kind, j, z, k)
-            src = w_own.at[at[1], at[2]]
-            mine = y % 2 == j
-            push(src, wb.at[at], sem_w.at[late, kind, j, k, 0], dev(x, rel(y, 1), z, core), mine)
-            push(src, wb.at[at], sem_w.at[late, kind, j, k, 0], dev(x, rel(y, 3), z, core), mine)
+        at = w_part(kind, y % 2, z, k)
+        src = w_own.at[at[1], at[2]]
+        push(src, wb.at[at], sem_w.at[kind, y % 2, k, 0], dev(x, rel(y, 1), z, core))
+        push(src, wb.at[at], sem_w.at[kind, y % 2, k, 0], dev(x, rel(y, 3), z, core))
 
     away = [lax.rem(y - 2 * k - j + 4, 4) for j in (0, 1)]
     foreign = [step != 0 for step in away]
 
-    def w_near(late, kind):
-        for j in (0,) if late else (0, 1):
+    def w_near(kind):
+        for j in (0, 1):
             near = (away[j] == 1) | (away[j] == 3)
             for part in (0, 1):
-                sems = sem_w.at[late, kind, j, part]
-                arrived(wb.at[w_part(late, kind, j, z, part)], sems.at[0], near)
-                half = wb.at[w_part(late, kind, j, z, part, 0)]
+                sems = sem_w.at[kind, j, part]
+                arrived(wb.at[w_part(kind, j, z, part)], sems.at[0], near)
+                half = wb.at[w_part(kind, j, z, part, 0)]
                 push(half, half, sems.at[0], y_next, away[j] == 1)
-                half = wb.at[w_part(late, kind, j, z, part, 1)]
+                half = wb.at[w_part(kind, j, z, part, 1)]
                 push(half, half, sems.at[1], y_prev, away[j] == 3)
                 if kind == 0:
-                    w_along_z(late, j, part, near)
-
-    def w_far(late, kind):
-        for j in (0,) if late else (0, 1):
+                    w_along_z(j, part, near)
+
+    def w_far(kind):
+        for j in (0, 1):
             far = away[j] == 2
             for part in (0, 1):
                 for half in (0, 1):
                     arrived(
-                        wb.at[w_part(late, kind, j, z, part, half)],
-                        sem_w.at[late, kind, j, part, half],
+                        wb.at[w_part(kind, j, z, part, half)],
+                        sem_w.at[kind, j, part, half],
                         far,
                     )
                 if kind == 0:
-                    w_along_z(late, j, part, far)
-
-    def w_along_z(late, j, part, when):
-        block = wb.at[w_part(late, 0, j, z, part)]
-        push(block, block, sem_wz.at[late, 0, j, part], z_next, when)
-        push(block, block, sem_wz.at[late, 1, j, part], z_prev, when)
-
-    def w_middle(late):
-        for j in (0,) if late else (0, 1):
+                    w_along_z(j, part, far)
+
+    def w_along_z(j, part, when):
+        block = wb.at[w_part(0, j, z, part)]
+        push(block, block, sem_wz.at[0, j, part], z_next, when)
+        push(block, block, sem_wz.at[1, j, part], z_prev, when)
+
+    def w_middle():
+        for j in (0, 1):
             for part in (0, 1):
-                from_left = wb.at[w_part(late, 0, j, zl, part)]
-                from_right = wb.at[w_part(late, 0, j, zr, part)]
-                arrived(from_left, sem_wz.at[late, 0, j, part], foreign[j])
-                arrived(from_right, sem_wz.at[late, 1, j, part], foreign[j])
+                from_left = wb.at[w_part(0, j, zl, part)]
+                from_right = wb.at[w_part(0, j, zr, part)]
+                arrived(from_left, sem_wz.at[0, j, part], foreign[j])
+                arrived(from_right, sem_wz.at[1, j, part], foreign[j])
                 if part == 0:
-                    push(from_left, from_left, sem_wz.at[late, 2, j, 0], z_next, foreign[j])
+                    push(from_left, from_left, sem_wz.at[2, j, 0], z_next, foreign[j])
                 else:
-                    push(from_right, from_right, sem_wz.at[late, 2, j, 1], z_prev, foreign[j])
-
-    def w_end(late):
-        for j in (0,) if late else (0, 1):
+                    push(from_right, from_right, sem_wz.at[2, j, 1], z_prev, foreign[j])
+
+    def w_end():
+        for j in (0, 1):
             for part in (0, 1):
                 arrived(
-                    wb.at[w_part(late, 0, j, zo, part)], sem_wz.at[late, 2, j, part], foreign[j]
+                    wb.at[w_part(0, j, zo, part)], sem_wz.at[2, j, part], foreign[j]
                 )
 
-    def o_part(y_, plane, core, half=None):
-        start, size = plane * 1024 + core * 512, 512
+    def o_part(kind, y_, plane, core, half=None):
+        if kind == 0:
+            start, size = (plane * 2 + core) * O_SPREAD, O_SPREAD
+        else:
+            start, size = 8 * O_SPREAD + core * O_DIRECT, O_DIRECT
         if half is not None:
-            start, size = start + half * 256, 256
-        return wo.at[y_, pl.ds(pl.multiple_of(start, 256), size), :]
-
-    def o_send():
+            start, size = start + half * (size // 2), size // 2
+        return (y_, pl.ds(pl.multiple_of(start, 64), size), slice(None))
+
+    others = [rel(y, step) for step in (1, 2, 3)]
+
+    def o_send(kind):
+        at = o_part(kind, y, z, k)
         for step in (1, 3, 2):
-            push(
-                w_out.at[pl.ds(pl.multiple_of(z * 1024 + k * 512, 512), 512), :],
-                o_part(y, z, k),
-                sem_wo.at[y],
-                dev(x, rel(y, step), z, k),
-            )
-
-    others = [rel(y, step) for step in (1, 2, 3)]
-
-    def o_along_z():
+            push(w_out.at[at[1], :], wo.at[at], sem_wo.at[kind, y], dev(x, rel(y, step), z, k))
+
+    def o_got(kind):
         for index, y_ in enumerate(others):
-            block = o_part(y_, z, k)
-            arrived(block, sem_wo.at[y_])
-            push(block, block, sem_woz.at[0, index], z_next)
-            push(block, block, sem_woz.at[1, index], z_prev)
-            push(block, block, sem_wos.at[0, index], sib)
+            block = wo.at[o_part(kind, y_, z, k)]
+            arrived(block, sem_wo.at[kind, y_])
+            if kind == 0:
+                push(block, block, sem_woz.at[0, index], z_next)
+                push(block, block, sem_woz.at[1, index], z_prev)
+            push(block, block, sem_wos.at[4 * kind, index], sib)
+
+    def o_middle():
+        for index, y_ in enumerate(others):
+            block = wo.at[o_part(0, y_, zl, k)]
+            arrived(block, sem_woz.at[0, index])
+            half = wo.at[o_part(0, y_, zl, k, 0)]
+            push(half, half, sem_woz.at[2, index], z_next)
+            push(block, block, sem_wos.at[1, index], sib)
+            block = wo.at[o_part(0, y_, zr, k)]
+            arrived(block, sem_woz.at[1, index])
+            half = wo.at[o_part(0, y_, zr, k, 1)]
+            push(half, half, sem_woz.at[3, index], z_prev)
+            push(block, block, sem_wos.at[2, index], sib)
+
+    def o_end():
+        for index, y_ in enumerate(others):
+            arrived(wo.at[o_part(0, y_, zo, k, 0)], sem_woz.at[2, index])
+            arrived(wo.at[o_part(0, y_, zo, k, 1)], sem_woz.at[3, index])
+            block = wo.at[o_part(0, y_, zo, k)]
+            push(block, block, sem_wos.at[3, index], sib)
+
+    def o_wait():
+        o_local.wait()
+        for index, y_ in enumerate(others):
+            for at, plane in enumerate((z, zl, zr, zo)):
+                arrived(wo.at[o_part(0, y_, plane, 1 - k)], sem_wos.at[at, index])
+            arrived(wo.at[o_part(1, y_, z, 1 - k)], sem_wos.at[4, index])
 
     def norm(block, piece, scale):
         wide = xb[block, piece].astype(F32).reshape(2 * PIECE, 1024)
@@ -377,48 +402,39 @@
             queries = queries + dot(normed, wb[0, block * 1024 : block * 1024 + 1024, :KEY])
         spread(qs, piece, queries.astype(BF16))
 
-    w_send(0, 0)
+    w_send(0)
     for copy in copies:
         copy.wait()
     pl.when(k == y // 2)(w_local.start)
     o_local.start()
     look_and_send(0)
     look_and_send(1)
-    w_near(0, 0)
+    w_near(0)
     look_and_send(2)
     ring_start(0)
     look_and_send(3)
-    w_far(0, 0)
-    w_send(0, 1)
+    w_far(0)
+    w_send(1)
     ring_start(1)
     ring_start(2)
     ring_middle(0)
     ring_start(3)
     ring_middle(1)
-    w_near(0, 1)
-    w_send(1, 0)
-    w_send(1, 1)
-    w_middle(0)
+    w_near(1)
+    w_middle()
     ring_middle(2)
     ring_end(0)
     ring_middle(3)
     ring_end(1)
-    w_far(0, 1)
-    o_send()
-    w_near(1, 0)
-    w_near(1, 1)
+    w_far(1)
     pl.when(k == y // 2)(w_local.wait)
-    w_end(0)
+    w_end()
     project(0)
     ring_end(2)
     project(1)
-    w_far(1, 0)
     ring_end(3)
     project(2)
     project(3)
-    w_middle(1)
-    w_far(1, 1)
-    o_along_z()
 
     head = 2 * x + k
     gates = gs[...]
@@ -460,9 +476,7 @@
     push(sum_aux.at[par], sum_aux.at[par], sem_mate.at[0], mate)
     push(sum_c.at[par], sum_c.at[par], sem_mate.at[1], mate)
 
-    w_end(1)
-    for piece in range(PIECES):
-        project_queries(piece)
+    o_send(0)
 
     lead_row = rows_in[8:9, :]
 
@@ -506,6 +520,9 @@
         to = dev(x, y, rel(z, step), k)
         push(pair_aux.at[z], pair_aux.at[z], sem_pair.at[0, z], to)
         push(pair_c.at[z], pair_c.at[z], sem_pair.at[1, z], to)
+    o_send(1)
+    for piece in range(PIECES):
+        project_queries(piece)
     for index in range(4):
         within(index)
 
@@ -514,14 +531,7 @@
         arrived(pair_aux.at[z_], sem_pair.at[0, z_])
         arrived(pair_c.at[z_], sem_pair.at[1, z_])
 
-    for index, y_ in enumerate(others):
-        from_left, from_right = o_part(y_, zl, k), o_part(y_, zr, k)
-        arrived(from_left, sem_woz.at[0, index])
-        arrived(from_right, sem_woz.at[1, index])
-        half = o_part(y_, zl, k, 0)
-        push(half, half, sem_woz.at[2, index], z_next)
-        half = o_part(y_, zr, k, 1)
-        push(half, half, sem_woz.at[3, index], z_prev)
+    o_got(0)
 
     def pairs(limit):
         return lax.fori_loop(
@@ -539,7 +549,7 @@
     memory_in = state_c[...].astype(BF16)
 
     def finish(start):
-        rows = pl.ds(pl.multiple_of(start, TILE), TILE)
+        rows = pl.ds(pl.multiple_of(start, PIECE), PIECE)
         q = qs[rows, :]
         carried = dot(q, memory_in) * 0.0625
         carried_norm = jnp.sum(q.astype(F32) * norm_in, axis=1, keepdims=True) * 0.0625
@@ -554,83 +564,69 @@
         scale = lax.rsqrt(jnp.mean(hidden * hidden, axis=1, keepdims=True) + epsilon)
         return (hidden * scale * gain).astype(BF16)
 
-    def act_of(block, kk, tile, half=None):
-        start, size = tile * TILE, TILE
-        if half is not None:
-            start, size = start + half * (TILE // 2), TILE // 2
-        return act.at[block, kk, pl.ds(start, size), :]
-
-    def act_start(kk, order, tile):
-        block = act_of(x, kk, tile)
-        push(block, block, sem_act.at[0, order, tile], x_next)
-        push(block, block, sem_act.at[1, order, tile], x_prev)
-
-    for tile in (0, 1):
-        act[x, k, tile * TILE : (tile + 1) * TILE, :] = finish(k_half + tile * TILE)
-        act_start(k, 0, tile)
-    for tile in (0, 1):
-        rows = slice(tile * TILE, (tile + 1) * TILE)
-        hn[rows, :] = finish((1 - k) * HALF + tile * TILE)
-        push(hn.at[rows, :], act_of(x, k, tile), sem_hn.at[tile], sib)
-    for tile in (0, 1):
-        arrived(act_of(x, 1 - k, tile), sem_hn.at[tile])
-        act_start(1 - k, 1, tile)
-
-    for index, y_ in enumerate(others):
-        block = o_part(y_, zl, k)
-        push(block, block, sem_wos.at[1, index], sib)
-        block = o_part(y_, zr, k)
-        push(block, block, sem_wos.at[2, index], sib)
-        arrived(o_part(y_, zo, k, 0), sem_woz.at[2, index])
-        arrived(o_part(y_, zo, k, 1), sem_woz.at[3, index])
-        block = o_part(y_, zo, k)
-        push(block, block, sem_wos.at[3, index], sib)
-
-    for order, kk in ((0, k), (1, 1 - k)):
-        for tile in (0, 1):
-            arrived(act_of(xl, kk, tile), sem_act.at[0, order, tile])
-            half = act_of(xl, kk, tile, 0)
-            push(half, half, sem_act.at[2, order, tile], x_next)
-            arrived(act_of(xr, kk, tile), sem_act.at[1, order, tile])
-            half = act_of(xr, kk, tile, 1)
-            push(half, half, sem_act.at[3, order, tile], x_prev)
+    def act_start(tile):
+        arrived(act.at[x, tile, 1 - k], sem_hn.at[tile])
+        block = act.at[x, tile]
+        push(block, block, sem_act.at[0, tile], x_next)
+        push(block, block, sem_act.at[1, tile], x_prev)
+
+    def act_middle(tile):
+        arrived(act.at[xl, tile], sem_act.at[0, tile])
+        push(act.at[xl, tile, 0], act.at[xl, tile, 0], sem_act.at[2, tile], x_next)
+        arrived(act.at[xr, tile], sem_act.at[1, tile])
+        push(act.at[xr, tile, 1], act.at[xr, tile, 1], sem_act.at[3, tile], x_prev)
+
+    for tile in range(PIECES):
+        hn[tile] = finish((1 - k) * HALF + tile * PIECE)
+        push(hn.at[tile], act.at[x, tile, k], sem_hn.at[tile], sib)
+        act[x, tile, k] = finish(k_half + tile * PIECE)
+        if tile > 0:
+            act_start(tile - 1)
+    act_start(PIECES - 1)
+    act_middle(0)
+    act_middle(1)
+    o_middle()
+    act_middle(2)
+    o_got(1)
+    act_middle(3)
 
     _, top_end, norm_end = pairs(4)
     aux_out[...] = jnp.where(row == 0, norm_end, top_end)
     keep_here = (k == req) & (par == k)
     mem_to = dev(x, 2 * k + req, z, par)
-    push(state_c, mem_got, sem_mem.at[0], mem_to, jnp.logical_not(keep_here))
+    mem_out[...] = state_c[...].astype(BF16)
+    push(mem_out, mem_got, sem_mem.at[0], mem_to, jnp.logical_not(keep_here))
     push(aux_out, aux_got, sem_mem.at[1], mem_to, jnp.logical_not(keep_here))
-    here(state_c, mem_got, sem_mem.at[0], keep_here)
+    here(mem_out, mem_got, sem_mem.at[0], keep_here)
     here(aux_out, aux_got, sem_mem.at[1], keep_here)
 
-    o_local.wait()
-    for index, y_ in enumerate(others):
-        for at, plane in enumerate((z, zl, zr, zo)):
-            arrived(o_part(y_, plane, 1 - k), sem_wos.at[at, index])
-
-    def mixed(block, tile, y_):
-        rows = slice(tile * TILE, (tile + 1) * TILE)
+    o_end()
+    o_wait()
+
+    def mixed(block, tiles, y_):
         start = pl.multiple_of(block * 1024, 1024)
-        return dot(act[block, 0, rows, :], wo[y_, pl.ds(start, 512), :]) + dot(
-            act[block, 1, rows, :], wo[y_, pl.ds(start + 512, 512), :]
+        first = act[block, tiles, 0].reshape(-1, VAL)
+        second = act[block, tiles, 1].reshape(-1, VAL)
+        return dot(first, wo[y_, pl.ds(start, 512), :]) + dot(
+            second, wo[y_, pl.ds(start + 512, 512), :]
         )
 
-    for tile in (0, 1):
+    for half in (0, 1):
+        tiles = pl.ds(half * 2, 2)
         for y_ in range(4):
-            own_p[tile * TILE : (tile + 1) * TILE, y_ * 256 : y_ * 256 + 256] = (
-                mixed(x, tile, y_) + mixed(xl, tile, y_) + mixed(xr, tile, y_)
+            own_p[half * TILE : (half + 1) * TILE, y_ * 256 : y_ * 256 + 256] = (
+                mixed(x, tiles, y_) + mixed(xl, tiles, y_) + mixed(xr, tiles, y_)
             )
-    for tile in (0, 1):
-        rows = slice(tile * TILE, (tile + 1) * TILE)
-        for order, kk in ((0, k), (1, 1 - k)):
-            for half in (0, 1):
-                arrived(act_of(xo, kk, tile, half), sem_act.at[2 + half, order, tile])
+    for tile in range(PIECES):
+        rows = slice(tile * PIECE, (tile + 1) * PIECE)
+        arrived(act.at[xo, tile, 0], sem_act.at[2, tile])
+        arrived(act.at[xo, tile, 1], sem_act.at[3, tile])
         for y_ in range(4):
             cols = slice(y_ * 256, y_ * 256 + 256)
-            total[rows, cols] = (own_p[rows, cols] + mixed(xo, tile, y_)).astype(BF16)
+            value = own_p[rows, cols] + mixed(xo, pl.ds(tile, 1), y_)
+            total[rows, cols] = value.astype(BF16)
             src = total.at[rows, cols]
-            dst = rows_got.at[req, pl.ds(pl.multiple_of(k_half + tile * TILE, TILE), TILE), :]
+            dst = rows_got.at[req, pl.ds(pl.multiple_of(k_half + tile * PIECE, PIECE), PIECE), :]
             mine = (y == y_) & (par == k)
             push(src, dst, sem_out.at[tile, req, k], dev(x, y_, z, par), jnp.logical_not(mine))
             here(src, dst, sem_out.at[tile, req, k], mine)
@@ -638,12 +634,12 @@
     arrived(mem_got, sem_mem.at[0])
     arrived(aux_got, sem_mem.at[1])
     keep = jnp.where(owner[h] == c, 1.0, 0.0)
-    out_mem[...] = mem_got[...] * keep
+    out_mem[...] = mem_got[...].astype(F32) * keep
     out_aux[...] = aux_got[...] * keep
-    for tile in (0, 1):
+    for tile in range(PIECES):
         for r_ in (0, 1):
             for k_ in (0, 1):
-                rows = slice(k_ * HALF + tile * TILE, k_ * HALF + (tile + 1) * TILE)
+                rows = slice(k_ * HALF + tile * PIECE, k_ * HALF + (tile + 1) * PIECE)
                 arrived(rows_got.at[r_, rows, :], sem_out.at[tile, r_, k_])
                 out[r_, rows, :] = (
                     emb[r_, rows, :].astype(F32) + rows_got[r_, rows, :].astype(F32)
@@ -697,12 +693,13 @@
             pltpu.VMEM((4, KEY, VAL), BF16),
             pltpu.VMEM((4, 8, KEY), F32),
             pltpu.VMEM((KEY, VAL), F32),
-            pltpu.VMEM((HALF, VAL), BF16),
-            pltpu.VMEM((4, 2, HALF, VAL), BF16),
+            pltpu.VMEM((PIECES, PIECE, VAL), BF16),
+            pltpu.VMEM((4, PIECES, 2, PIECE, VAL), BF16),
             pltpu.VMEM((HALF, 1024), F32),
             pltpu.VMEM((HALF, 1024), BF16),
             pltpu.VMEM((2, ROWS, 256), BF16),
-            pltpu.VMEM((KEY, VAL), F32),
+            pltpu.VMEM((KEY, VAL), BF16),
+            pltpu.VMEM((KEY, VAL), BF16),
             pltpu.VMEM((8, KEY), F32),
             pltpu.VMEM((8, KEY), F32),
             dma((SENDS,)),
@@ -711,16 +708,16 @@
             dma((PIECES, 4)),
             dma((4, PIECES)),
             dma((4, PIECES)),
-            dma((2, 2, 2, 2, 2)),
-            dma((2, 3, 2, 2)),
-            dma((4,)),
+            dma((2, 2, 2, 2)),
+            dma((3, 2, 2)),
+            dma((2, 4)),
             dma((4, 3)),
-            dma((4, 3)),
+            dma((5, 3)),
             dma((2,)),
             dma((2, 4)),
-            dma((2,)),
-            dma((4, 2, 2)),
-            dma((2, 2, 2)),
+            dma((PIECES,)),
+            dma((4, PIECES)),
+            dma((PIECES, 2, 2)),
             dma((2,)),
         ],
         compiler_params=pltpu.CompilerParams(

time: 170 us -> 151 us (0.89)
  Pallas kernels: 166 us -> 148 us
    pallas_call x1, Pallas kernels: 163 us -> 146 us  [local(): pl.pallas_call(kernel, out_shape=(jax.ShapeDtypeStruct((2, ROWS, 256), BF...]
where the time goes in v5:
time: 151 us; the launch traced here: 150 us
  Pallas kernels  148 us (98%)
    pallas_call x1, Pallas kernels, local(): pl.pallas_call(kernel, out_shape=(jax.ShapeDtypeStruct((2, ROWS, 256), BF...  146 us

profile of v5, /device:TPU:8, one launch (start us, length us, event | category | flops | bytes accessed | tf_op | source)
XLA Modules:
  0.0 150.2 jit_solution(7217573262675194759)
XLA Ops:
  0.6 1.3 reshape.28.norm_gain
  1.9 145.6 %shard_map.120 = (bf16[2,1024,256]{2,1,0:T(8,128)(2,1)}, f32[256,512]{1,0:T(8,128)}, f32[8,256]{1,0:T(8,128)}) custom-call(s32[2,1024]{1,0:T(2,128)} %ids.1, bf16[4096,8,256]{2,1,0:T(8,128)(2,1)} %bitcast.8, bf16[4096,512]{1,0:T(8,128)(2,1)} %bitcast.9, bf16[4096,256]{1,0:T(8,128)(2,1)} %w_out.1, bf16[16,4096]{1,0:T(8,128)(2,1)} %bitcast.10, ...), custom_call_target="tpu_custom_call" | custom-call | tf_op jit(solution)/shard_map/pallas_call | solution.py:667
  147.6 2.6 %shard_map.121 = (bf16[2,1024,256]{2,1,0:T(8,128)(2,1)}, f32[256,512]{1,0:T(8,128)}, f32[1,256]{1,0:T(1,128)}, f32[1,1]{1,0:T(1,128)}) custom-call(bf16[2,1024,256]{2,1,0:T(8,128)(2,1)} %get-tuple-element.11.rows, f32[256,512]{1,0:T(8,128)} %get-tuple-element.12.mem, f32[8,256]{1,0:T(8,128)} %get-tuple-element.13.aux), custom_call_target="tpu_custom_call" | custom-call | tf_op jit(solution)/shard_map/pallas_call | solution.py:737

commit v6 on v5

--- a/solution.py
+++ b/solution.py
@@ -19,8 +19,8 @@
 KEY = 256
 VAL = 512
 SENDS = 192
-SPREAD = 320
-DIRECT = 768
+SPREAD = 384
+DIRECT = 512
 O_SPREAD = 256
 O_DIRECT = 1024
 TILE = 256
@@ -371,7 +371,7 @@
             start = core * HALF + piece * PIECE
             target[start : start + PIECE, :] = value[core * PIECE : (core + 1) * PIECE, :]
 
-    def project(piece):
+    def prepare(piece):
         for index, block_x in enumerate((x, xl, xr, xo)):
             arrived(rows_of(block_x, 1 - k, piece), sem_sib.at[index, piece])
         squares = jnp.zeros((2 * PIECE, 1), F32)
@@ -380,6 +380,9 @@
             squares += jnp.sum(wide * wide, axis=1, keepdims=True)
         scale = lax.rsqrt(squares / WIDTH + epsilon)
         scales[piece] = jnp.broadcast_to(scale, (2 * PIECE, 128))
+
+    def project(piece):
+        scale = scales[piece][:, 0:1]
         keys, values = jnp.zeros((2 * PIECE, KEY), F32), jnp.zeros((2 * PIECE, VAL), F32)
         gate = jnp.zeros((16, 2 * PIECE), F32)
         for block in range(4):
@@ -420,19 +423,23 @@
     ring_middle(0)
     ring_start(3)
     ring_middle(1)
-    w_near(1)
     w_middle()
     ring_middle(2)
+    w_near(1)
     ring_end(0)
     ring_middle(3)
     ring_end(1)
+    prepare(0)
+    prepare(1)
+    ring_end(2)
+    prepare(2)
     w_far(1)
     pl.when(k == y // 2)(w_local.wait)
     w_end()
     project(0)
-    ring_end(2)
     project(1)
     ring_end(3)
+    prepare(3)
     project(2)
     project(3)
 

time: 151 us -> 151 us (level); the launches traced: 150 us -> 148 us
  Pallas kernels: 148 us -> 146 us
    pallas_call x1, Pallas kernels: 146 us -> 144 us  [local(): pl.pallas_call(kernel, out_shape=(jax.ShapeDtypeStruct((2, ROWS, 256), BF...]
where the time goes in v6:
time: 151 us; the launch traced here: 148 us
  Pallas kernels  146 us (97%)
    pallas_call x1, Pallas kernels, local(): pl.pallas_call(kernel, out_shape=(jax.ShapeDtypeStruct((2, ROWS, 256), BF...  144 us

profile of v6, /device:TPU:8, one launch (start us, length us, event | category | flops | bytes accessed | tf_op | source)
XLA Modules:
  0.0 148.2 jit_solution(9635221696619298036)
XLA Ops:
  0.6 1.3 reshape.28.norm_gain
  1.9 143.7 %shard_map.120 = (bf16[2,1024,256]{2,1,0:T(8,128)(2,1)}, f32[256,512]{1,0:T(8,128)}, f32[8,256]{1,0:T(8,128)}) custom-call(s32[2,1024]{1,0:T(2,128)} %ids.1, bf16[4096,8,256]{2,1,0:T(8,128)(2,1)} %bitcast.8, bf16[4096,512]{1,0:T(8,128)(2,1)} %bitcast.9, bf16[4096,256]{1,0:T(8,128)(2,1)} %w_out.1, bf16[16,4096]{1,0:T(8,128)(2,1)} %bitcast.10, ...), custom_call_target="tpu_custom_call" | custom-call | tf_op jit(solution)/shard_map/pallas_call | solution.py:674
  145.6 2.6 %shard_map.121 = (bf16[2,1024,256]{2,1,0:T(8,128)(2,1)}, f32[256,512]{1,0:T(8,128)}, f32[1,256]{1,0:T(1,128)}, f32[1,1]{1,0:T(1,128)}) custom-call(bf16[2,1024,256]{2,1,0:T(8,128)(2,1)} %get-tuple-element.11.rows, f32[256,512]{1,0:T(8,128)} %get-tuple-element.12.mem, f32[8,256]{1,0:T(8,128)} %get-tuple-element.13.aux), custom_call_target="tpu_custom_call" | custom-call | tf_op jit(solution)/shard_map/pallas_call | solution.py:744
